TPU v7x, 32 devices: a whole 2x2x4 slice. The times are simulated.
32 devices in a mesh: ctx: 16 (over z, y, x), tp: 2 (over core).
Axes of the slice: x: 2, y: 2, z: 4, core: 2. Of those that a mesh axis runs over, the one named last changes fastest.
Arguments:
- features: bfloat16 [3, 1024, 8192], P(None, 'ctx', 'tp'), may hold values from -6 to 6
- short_weight: float32 [3, 3, 8192], P(None, None, 'tp'), may hold values from -3 to 3
- decay_rate: float32 [512, 16], P('tp'), may hold values from 0.00048828125 to 0.03
- residue: float32 [512, 16], P('tp'), may hold values from -3 to 3
- skip_gain: float32 [8192], P('tp'), may hold values from -1 to 1
- out_weight: bfloat16 [8192, 4096], P('tp', 'ctx'), may hold values from -0.09375 to 0.09375
Outputs:
- mixed_out: bfloat16 [1024, 4096], P('ctx', 'tp')
All inputs are finite; a program needn't handle non-finite values.
Results may differ from a plain program's by a relative error of at most 0.006.
Values may be sent and summed in bfloat16 or wider, within the bound.
A program may use at most 128 MiB of HBM per device.

v0:
```python
import math

import jax
import jax.numpy as jnp
from jax import lax
from jax.sharding import PartitionSpec as P


def passed_along(shard, axis, by):
    length = lax.axis_size(axis)
    pairs = [(i, i + by) for i in range(length) if 0 <= i + by < length]
    return lax.ppermute(shard, axis, pairs)


def entering(value, axis, join, neutral):
    count, mine = (lax.axis_size(axis), lax.axis_index(axis))
    pieces = jax.tree.map(lambda part: lax.all_gather(part, axis), value)
    running = jax.tree.map(
        lambda part, zero: jnp.full_like(part, 0) + jnp.asarray(zero, part.dtype), value, neutral
    )

    def hop(position, running):
        longer = join(running, jax.tree.map(lambda part: part[position], pieces))
        return jax.tree.map(lambda new, old: jnp.where(position < mine, new, old), longer, running)

    return lax.fori_loop(0, count - 1, hop, running)


def combine_states(earlier, later):
    return (earlier[0] * later[0], later[1] + later[0][:, None, :] * earlier[1])


def per_device(features, short_weight, decay_rate, residue, skip_gain, out_weight):
    hi = lax.Precision.HIGHEST
    rows = features.shape[1]
    chans = features.shape[2]
    groups = decay_rate.shape[0]
    modes = decay_rate.shape[1]
    width = chans // groups
    taps = short_weight.shape[1]
    rim = passed_along(features[:, rows - (taps - 1) :, :], "ctx", 1)
    extended = jnp.concatenate([rim, features], axis=1)
    conv = jnp.zeros(features.shape, jnp.float32)
    for j in range(taps):
        conv = conv + short_weight[:, j][:, None, :] * extended[
            :, taps - 1 - j : taps - 1 - j + rows, :
        ].astype(jnp.float32)
    q_lane = conv[0]
    gated = (conv[1] * conv[2]).astype(jnp.bfloat16)
    coef = residue * jnp.sqrt(-jnp.expm1(-2.0 * decay_rate))
    lags = jnp.arange(rows, dtype=jnp.float32)
    near_filter = jnp.sum(
        coef[:, :, None] * jnp.exp(-decay_rate[:, :, None] * lags[None, None, :]), axis=1
    ).astype(jnp.bfloat16)
    index = jnp.arange(rows, dtype=jnp.int32)
    offset = index[:, None] - index[None, :]
    lower = offset >= 0
    clipped = jnp.clip(offset, 0, rows - 1)
    gstep = math.gcd(groups, 8)
    nblock = groups // gstep
    filter_blocks = near_filter.reshape(nblock, gstep, rows)
    input_blocks = gated.reshape(rows, nblock, gstep, width).transpose(1, 0, 2, 3)

    def near_block(pair):
        taps_here, inputs_here = pair
        toeplitz = jnp.where(lower[None], taps_here[:, clipped], jnp.zeros((), jnp.bfloat16))
        return jnp.einsum("gts,sgw->tgw", toeplitz, inputs_here, preferred_element_type=jnp.float32)

    near = (
        lax.map(near_block, (filter_blocks, input_blocks))
        .transpose(1, 0, 2, 3)
        .reshape(rows, chans)
    )
    gated_wide = gated.astype(jnp.float32)
    grouped = gated_wide.reshape(rows, groups, width)
    end_basis = jnp.exp(-decay_rate[None] * (rows - 1.0 - lags)[:, None, None])
    own_state = jnp.einsum("tgs,tgw->gws", end_basis, grouped, precision=hi)
    block_decay = jnp.exp(-decay_rate * rows)
    identity = (
        jnp.ones((groups, modes), jnp.float32),
        jnp.zeros((groups, width, modes), jnp.float32),
    )
    incoming = entering((block_decay, own_state), "ctx", combine_states, identity)[1]
    far_basis = coef[None] * jnp.exp(-decay_rate[None] * (lags + 1.0)[:, None, None])
    far = jnp.einsum("tgs,gws->tgw", far_basis, incoming, precision=hi).reshape(rows, chans)
    mixed = (q_lane * (near + far + skip_gain[None, :] * gated_wide)).astype(jnp.bfloat16)
    partial_out = jnp.dot(
        mixed,
        lax.all_gather(out_weight, "ctx", axis=1, tiled=True),
        preferred_element_type=jnp.float32,
    )
    return lax.psum_scatter(partial_out, "tp", scatter_dimension=1, tiled=True).astype(jnp.bfloat16)


def solution(mesh):
    placed = (
        P(None, "ctx", "tp"),
        P(None, None, "tp"),
        P("tp", None),
        P("tp", None),
        P("tp"),
        P("tp", "ctx"),
    )
    return jax.shard_map(
        per_device, mesh=mesh, in_specs=placed, out_specs=P("ctx", "tp"), check_vma=False
    )
```

profile of v0, /device:TPU:1, one launch (start us, length us, event | category | flops | bytes accessed | tf_op | source)
XLA Modules:
  0.0 829.5 jit_solution(13102797324867995350)
XLA Ops:
  25.8 35.3 %all-gather.1 = f32[4096,16]{0,1:T(8,128)S(1)} all-gather(f32[256,16]{0,1:T(8,128)S(1)} %get-tuple-element.215), channel_id=3, replica_groups=mesh['ctx'=16,'tp'=2] {'ctx'}, dimensions={0}, use_global_device_ids=true | all-gather | bytes 278528 | tf_op jit(solution)/shard_map/all_gather | solution.py:17
  61.6 458.7 %while.25 = (s32[]{:T(128)}, f32[32,64,8,16]{1,3,2,0:T(8,128)}, bf16[32,64,8,16]{1,3,2,0:T(8,128)(2,1)}, bf16[32,8,64]{2,1,0:T(8,128)(2,1)S(1)}, s32[]{:T(128)}) while((s32[]{:T(128)}, f32[32,64,8,16]{1,3,2,0:T(8,128)}, bf16[32,64,8,16]{1,3,2,0:T(8,128)(2,1)}, bf16[32,8,64]{2,1,0:T(8,128)(2,1)S(1)}, s32[]{:T(128)}) %tuple.75), condition=%wide.region_2.3_spmd.clone, body=%wide.region_1.2_spmd.clone.sunk | while | flops 1114114 | bytes 537665 | solution.py:70
  61.8 12.1 %gather_fusion = bf16[4096,8]{1,0:T(8,128)(2,1)S(1)} fusion(bf16[8,64]{0,1:T(8,128)(2,1)S(1)} %bitcast.87, s32[4096]{0:T(1024)S(1)} %broadcast_clamp_fusion.2), kind=kCustom, calls=%fused_computation.clone.clone.1 | custom fusion | bytes 147456 | tf_op jit(solution)/shard_map/while/body/eval_jaxpr/gather | solution.py:66
  76.2 12.1 %gather_fusion = bf16[4096,8]{1,0:T(8,128)(2,1)S(1)} fusion(bf16[8,64]{0,1:T(8,128)(2,1)S(1)} %bitcast.87, s32[4096]{0:T(1024)S(1)} %broadcast_clamp_fusion.2), kind=kCustom, calls=%fused_computation.clone.clone.1 | custom fusion | bytes 147456 | tf_op jit(solution)/shard_map/while/body/eval_jaxpr/gather | solution.py:66
  90.5 12.1 %gather_fusion = bf16[4096,8]{1,0:T(8,128)(2,1)S(1)} fusion(bf16[8,64]{0,1:T(8,128)(2,1)S(1)} %bitcast.87, s32[4096]{0:T(1024)S(1)} %broadcast_clamp_fusion.2), kind=kCustom, calls=%fused_computation.clone.clone.1 | custom fusion | bytes 147456 | tf_op jit(solution)/shard_map/while/body/eval_jaxpr/gather | solution.py:66
  104.8 12.1 %gather_fusion = bf16[4096,8]{1,0:T(8,128)(2,1)S(1)} fusion(bf16[8,64]{0,1:T(8,128)(2,1)S(1)} %bitcast.87, s32[4096]{0:T(1024)S(1)} %broadcast_clamp_fusion.2), kind=kCustom, calls=%fused_computation.clone.clone.1 | custom fusion | bytes 147456 | tf_op jit(solution)/shard_map/while/body/eval_jaxpr/gather | solution.py:66
  119.2 12.1 %gather_fusion = bf16[4096,8]{1,0:T(8,128)(2,1)S(1)} fusion(bf16[8,64]{0,1:T(8,128)(2,1)S(1)} %bitcast.87, s32[4096]{0:T(1024)S(1)} %broadcast_clamp_fusion.2), kind=kCustom, calls=%fused_computation.clone.clone.1 | custom fusion | bytes 147456 | tf_op jit(solution)/shard_map/while/body/eval_jaxpr/gather | solution.py:66
  133.5 12.1 %gather_fusion = bf16[4096,8]{1,0:T(8,128)(2,1)S(1)} fusion(bf16[8,64]{0,1:T(8,128)(2,1)S(1)} %bitcast.87, s32[4096]{0:T(1024)S(1)} %broadcast_clamp_fusion.2), kind=kCustom, calls=%fused_computation.clone.clone.1 | custom fusion | bytes 147456 | tf_op jit(solution)/shard_map/while/body/eval_jaxpr/gather | solution.py:66
  147.8 12.1 %gather_fusion = bf16[4096,8]{1,0:T(8,128)(2,1)S(1)} fusion(bf16[8,64]{0,1:T(8,128)(2,1)S(1)} %bitcast.87, s32[4096]{0:T(1024)S(1)} %broadcast_clamp_fusion.2), kind=kCustom, calls=%fused_computation.clone.clone.1 | custom fusion | bytes 147456 | tf_op jit(solution)/shard_map/while/body/eval_jaxpr/gather | solution.py:66
  162.2 12.1 %gather_fusion = bf16[4096,8]{1,0:T(8,128)(2,1)S(1)} fusion(bf16[8,64]{0,1:T(8,128)(2,1)S(1)} %bitcast.87, s32[4096]{0:T(1024)S(1)} %broadcast_clamp_fusion.2), kind=kCustom, calls=%fused_computation.clone.clone.1 | custom fusion | bytes 147456 | tf_op jit(solution)/shard_map/while/body/eval_jaxpr/gather | solution.py:66
  176.5 12.1 %gather_fusion = bf16[4096,8]{1,0:T(8,128)(2,1)S(1)} fusion(bf16[8,64]{0,1:T(8,128)(2,1)S(1)} %bitcast.87, s32[4096]{0:T(1024)S(1)} %broadcast_clamp_fusion.2), kind=kCustom, calls=%fused_computation.clone.clone.1 | custom fusion | bytes 147456 | tf_op jit(solution)/shard_map/while/body/eval_jaxpr/gather | solution.py:66
  190.8 12.1 %gather_fusion = bf16[4096,8]{1,0:T(8,128)(2,1)S(1)} fusion(bf16[8,64]{0,1:T(8,128)(2,1)S(1)} %bitcast.87, s32[4096]{0:T(1024)S(1)} %broadcast_clamp_fusion.2), kind=kCustom, calls=%fused_computation.clone.clone.1 | custom fusion | bytes 147456 | tf_op jit(solution)/shard_map/while/body/eval_jaxpr/gather | solution.py:66
  205.2 12.1 %gather_fusion = bf16[4096,8]{1,0:T(8,128)(2,1)S(1)} fusion(bf16[8,64]{0,1:T(8,128)(2,1)S(1)} %bitcast.87, s32[4096]{0:T(1024)S(1)} %broadcast_clamp_fusion.2), kind=kCustom, calls=%fused_computation.clone.clone.1 | custom fusion | bytes 147456 | tf_op jit(solution)/shard_map/while/body/eval_jaxpr/gather | solution.py:66
  219.5 12.1 %gather_fusion = bf16[4096,8]{1,0:T(8,128)(2,1)S(1)} fusion(bf16[8,64]{0,1:T(8,128)(2,1)S(1)} %bitcast.87, s32[4096]{0:T(1024)S(1)} %broadcast_clamp_fusion.2), kind=kCustom, calls=%fused_computation.clone.clone.1 | custom fusion | bytes 147456 | tf_op jit(solution)/shard_map/while/body/eval_jaxpr/gather | solution.py:66
  233.9 12.1 %gather_fusion = bf16[4096,8]{1,0:T(8,128)(2,1)S(1)} fusion(bf16[8,64]{0,1:T(8,128)(2,1)S(1)} %bitcast.87, s32[4096]{0:T(1024)S(1)} %broadcast_clamp_fusion.2), kind=kCustom, calls=%fused_computation.clone.clone.1 | custom fusion | bytes 147456 | tf_op jit(solution)/shard_map/while/body/eval_jaxpr/gather | solution.py:66
  248.2 12.1 %gather_fusion = bf16[4096,8]{1,0:T(8,128)(2,1)S(1)} fusion(bf16[8,64]{0,1:T(8,128)(2,1)S(1)} %bitcast.87, s32[4096]{0:T(1024)S(1)} %broadcast_clamp_fusion.2), kind=kCustom, calls=%fused_computation.clone.clone.1 | custom fusion | bytes 147456 | tf_op jit(solution)/shard_map/while/body/eval_jaxpr/gather | solution.py:66
  262.5 12.1 %gather_fusion = bf16[4096,8]{1,0:T(8,128)(2,1)S(1)} fusion(bf16[8,64]{0,1:T(8,128)(2,1)S(1)} %bitcast.87, s32[4096]{0:T(1024)S(1)} %broadcast_clamp_fusion.2), kind=kCustom, calls=%fused_computation.clone.clone.1 | custom fusion | bytes 147456 | tf_op jit(solution)/shard_map/while/body/eval_jaxpr/gather | solution.py:66
  276.9 12.1 %gather_fusion = bf16[4096,8]{1,0:T(8,128)(2,1)S(1)} fusion(bf16[8,64]{0,1:T(8,128)(2,1)S(1)} %bitcast.87, s32[4096]{0:T(1024)S(1)} %broadcast_clamp_fusion.2), kind=kCustom, calls=%fused_computation.clone.clone.1 | custom fusion | bytes 147456 | tf_op jit(solution)/shard_map/while/body/eval_jaxpr/gather | solution.py:66
  291.2 12.1 %gather_fusion = bf16[4096,8]{1,0:T(8,128)(2,1)S(1)} fusion(bf16[8,64]{0,1:T(8,128)(2,1)S(1)} %bitcast.87, s32[4096]{0:T(1024)S(1)} %broadcast_clamp_fusion.2), kind=kCustom, calls=%fused_computation.clone.clone.1 | custom fusion | bytes 147456 | tf_op jit(solution)/shard_map/while/body/eval_jaxpr/gather | solution.py:66
  305.5 12.1 %gather_fusion = bf16[4096,8]{1,0:T(8,128)(2,1)S(1)} fusion(bf16[8,64]{0,1:T(8,128)(2,1)S(1)} %bitcast.87, s32[4096]{0:T(1024)S(1)} %broadcast_clamp_fusion.2), kind=kCustom, calls=%fused_computation.clone.clone.1 | custom fusion | bytes 147456 | tf_op jit(solution)/shard_map/while/body/eval_jaxpr/gather | solution.py:66
  319.9 12.1 %gather_fusion = bf16[4096,8]{1,0:T(8,128)(2,1)S(1)} fusion(bf16[8,64]{0,1:T(8,128)(2,1)S(1)} %bitcast.87, s32[4096]{0:T(1024)S(1)} %broadcast_clamp_fusion.2), kind=kCustom, calls=%fused_computation.clone.clone.1 | custom fusion | bytes 147456 | tf_op jit(solution)/shard_map/while/body/eval_jaxpr/gather | solution.py:66
  334.2 12.1 %gather_fusion = bf16[4096,8]{1,0:T(8,128)(2,1)S(1)} fusion(bf16[8,64]{0,1:T(8,128)(2,1)S(1)} %bitcast.87, s32[4096]{0:T(1024)S(1)} %broadcast_clamp_fusion.2), kind=kCustom, calls=%fused_computation.clone.clone.1 | custom fusion | bytes 147456 | tf_op jit(solution)/shard_map/while/body/eval_jaxpr/gather | solution.py:66
  348.5 12.1 %gather_fusion = bf16[4096,8]{1,0:T(8,128)(2,1)S(1)} fusion(bf16[8,64]{0,1:T(8,128)(2,1)S(1)} %bitcast.87, s32[4096]{0:T(1024)S(1)} %broadcast_clamp_fusion.2), kind=kCustom, calls=%fused_computation.clone.clone.1 | custom fusion | bytes 147456 | tf_op jit(solution)/shard_map/while/body/eval_jaxpr/gather | solution.py:66
  362.9 12.1 %gather_fusion = bf16[4096,8]{1,0:T(8,128)(2,1)S(1)} fusion(bf16[8,64]{0,1:T(8,128)(2,1)S(1)} %bitcast.87, s32[4096]{0:T(1024)S(1)} %broadcast_clamp_fusion.2), kind=kCustom, calls=%fused_computation.clone.clone.1 | custom fusion | bytes 147456 | tf_op jit(solution)/shard_map/while/body/eval_jaxpr/gather | solution.py:66
  377.2 12.1 %gather_fusion = bf16[4096,8]{1,0:T(8,128)(2,1)S(1)} fusion(bf16[8,64]{0,1:T(8,128)(2,1)S(1)} %bitcast.87, s32[4096]{0:T(1024)S(1)} %broadcast_clamp_fusion.2), kind=kCustom, calls=%fused_computation.clone.clone.1 | custom fusion | bytes 147456 | tf_op jit(solution)/shard_map/while/body/eval_jaxpr/gather | solution.py:66
  391.5 12.1 %gather_fusion = bf16[4096,8]{1,0:T(8,128)(2,1)S(1)} fusion(bf16[8,64]{0,1:T(8,128)(2,1)S(1)} %bitcast.87, s32[4096]{0:T(1024)S(1)} %broadcast_clamp_fusion.2), kind=kCustom, calls=%fused_computation.clone.clone.1 | custom fusion | bytes 147456 | tf_op jit(solution)/shard_map/while/body/eval_jaxpr/gather | solution.py:66
  420.2 12.1 %gather_fusion = bf16[4096,8]{1,0:T(8,128)(2,1)S(1)} fusion(bf16[8,64]{0,1:T(8,128)(2,1)S(1)} %bitcast.87, s32[4096]{0:T(1024)S(1)} %broadcast_clamp_fusion.2), kind=kCustom, calls=%fused_computation.clone.clone.1 | custom fusion | bytes 147456 | tf_op jit(solution)/shard_map/while/body/eval_jaxpr/gather | solution.py:66
  434.5 12.1 %gather_fusion = bf16[4096,8]{1,0:T(8,128)(2,1)S(1)} fusion(bf16[8,64]{0,1:T(8,128)(2,1)S(1)} %bitcast.87, s32[4096]{0:T(1024)S(1)} %broadcast_clamp_fusion.2), kind=kCustom, calls=%fused_computation.clone.clone.1 | custom fusion | bytes 147456 | tf_op jit(solution)/shard_map/while/body/eval_jaxpr/gather | solution.py:66
  463.2 12.1 %gather_fusion = bf16[4096,8]{1,0:T(8,128)(2,1)S(1)} fusion(bf16[8,64]{0,1:T(8,128)(2,1)S(1)} %bitcast.87, s32[4096]{0:T(1024)S(1)} %broadcast_clamp_fusion.2), kind=kCustom, calls=%fused_computation.clone.clone.1 | custom fusion | bytes 147456 | tf_op jit(solution)/shard_map/while/body/eval_jaxpr/gather | solution.py:66
  529.4 30.6 %while.26 = (s32[]{:T(128)}, f32[256,16,16]{0,2,1:T(8,128)S(1)}, s32[]{:T(128)}, f32[16,256,16,16]{1,0,3,2:T(8,128)}, f32[16,256,16]{1,0,2:T(8,128)S(1)}, /*index=5*/s32[]{:T(128)}, s32[]{:T(128)}) while((s32[]{:T(128)}, f32[256,16,16]{0,2,1:T(8,128)S(1)}, s32[]{:T(128)}, f32[16,256,16,16]{1,0,3,2:T(8,128)}, ...), condition=%wide.region_4.5_spmd.clone, body=%wide.region_3.4_spmd.clone.sunk | while | flops 262148 | bytes 1392745 | solution.py:26
  567.5 225.3 %all-gather.5.cloned.1.call-done = bf16[4096,4096]{1,0:T(8,128)(2,1)} async-done(((bf16[4096,256]{1,0:T(8,128)(2,1)}), bf16[4096,4096]{1,0:T(8,128)(2,1)}) %all-gather.5.cloned.1.call-update) | async-done | bytes 33554448 | tf_op jit(solution)/shard_map/all_gather | solution.py:89
  792.8 17.8 %fusion.33 = f32[64,4096]{1,0:T(8,128)} fusion(bf16[4096,4096]{1,0:T(8,128)(2,1)} %all-gather.5.cloned.1.call-done, f32[3,64,4096]{2,1,0:T(8,128)} %copy-done, f32[64,4096]{1,0:T(8,128)S(1)} %copy-done.1, f32[64,4096]{1,0:T(8,128)S(1)} %copy.57, bf16[1,64,4096]{2,1,0:T(8,128)(2,1)S(1)} %fusion.24, f32[4096]{0:T(1024)S(1)} %copy-done.2), kind=kOutput, calls=%fused_computation.49 | convolution fusion | flops 2149056512 | bytes 38289408 | tf_op jit(solution)/shard_map/dot_general | solution.py:87
  (362 shorter events, 209.2 us)
Async XLA Ops:
  6.5 517.0 %all-gather.7.cloned.1.call-start = ((), (), s32[]{:S(2)}) async-start(), calls=%async_computation.3 | async-start | bytes 4456448 | tf_op jit(solution)/shard_map/all_gather | solution.py:17
  7.5 6.2 collective-permute-start
  16.9 1.6 copy-start
  25.0 767.8 %all-gather.5.cloned.1.call-start = ((), (), s32[]{:S(2)}) async-start(), calls=%async_computation.1 | async-start | bytes 35651584 | tf_op jit(solution)/shard_map/all_gather | solution.py:89
  25.7 795.5 %reduce-scatter.2.cloned.1.call-start = ((), (), s32[]{:S(2)}) async-start(), calls=%async_computation.2 | async-start | bytes 1572864 | tf_op jit(solution)/shard_map/reduce_scatter | solution.py:92
  565.3 227.5 %copy-start.1 = (f32[64,4096]{1,0:T(8,128)S(1)}, f32[64,4096]{1,0:T(8,128)}, u32[]{:S(2)}) copy-start(f32[64,4096]{1,0:T(8,128)} %copy.56) | copy-start | bytes 3145732
  565.3 227.5 %copy-start.2 = (f32[4096]{0:T(1024)S(1)}, f32[4096]{0:T(1024)}, u32[]{:S(2)}) copy-start(f32[4096]{0:T(1024)} %param.14) | copy-start | bytes 49156
Sparse Core Ops, SparseCore 0:
  25.1 83.8 all-gather.6
  110.5 682.3 all-gather.4
  810.7 10.3 reduce-scatter.1
where the time goes:
time: 833 us; the launch traced here: 829 us
  local copies, waits for them, and re-layouts  454 us (55%)
  waiting for transfers between devices  237 us (28%)
  matrix products  75.4 us (9%)
  blocking collectives  35.3 us (4%)
  between operations  13.2 us (2%)
  other arithmetic  9.06 us (1%)
    gather x64, local copies, waits for them, and re-layouts, near_block(): taps_here[:, clipped]  401 us
    all_gather x1, waiting for transfers between devices, per_device(): lax.all_gather(out_weight, 'ctx', axis=1, tiled=True)  225 us
    dot_general x32, matrix products, near_block(): jnp.einsum('gts,sgw->tgw', toeplitz, inputs_here, preferred_element_type=...  50.3 us
    all_gather x1, blocking collectives, entering(): pieces = jax.tree.map(lambda part: lax.all_gather(part, axis), value)  35.3 us
    dynamic_slice x45, local copies, waits for them, and re-layouts, hop(): longer = join(running, jax.tree.map(lambda part: part[position], pieces))  27.8 us
    dot_general x1, matrix products, per_device(): jnp.dot(mixed, lax.all_gather(out_weight, 'ctx', axis=1, tiled=True), pre...  17.8 us
  transfers between devices with their start and end apart: 4, of which 2 were waited for; matrix products, arithmetic and copies ran while one was open for 61% of the time, Pallas kernels for 0%

commit v1 on v0

v1 whole, which is shorter than its diff:
```python
import jax
import jax.numpy as jnp
from jax import lax
from jax.experimental import pallas as pl
from jax.experimental.pallas import tpu as pltpu
from jax.sharding import PartitionSpec as P

LANES = 128


def modal_sum(decay, weight, rows, shift):
    modes = decay.shape[0]
    lag = lax.broadcasted_iota(jnp.int32, (8, LANES), 0).astype(jnp.float32) + shift
    total = [jnp.zeros((8, LANES), jnp.float32) for _ in range(rows // 8)]
    for s in range(modes):
        rate = decay[s : s + 1]
        power = weight[s : s + 1] * jnp.exp(-rate * lag)
        stride = jnp.exp(-8.0 * rate)
        for b in range(rows // 8):
            total[b] = total[b] + power
            if b + 1 < rows // 8:
                power = power * stride
    return total


def front_kernel(x_ref, rim_ref, w_ref, decay_ref, coef_ref, skip_ref, q_ref, base_ref, state_ref, ext, filt, gate):
    rows = x_ref.shape[1]
    taps = w_ref.shape[1]
    modes = decay_ref.shape[0]
    nb = rows // 8

    def tile(i, carry):
        at = pl.ds(pl.multiple_of(i * LANES, LANES), LANES)
        conv = []
        for lane in range(3):
            ext[lane, 0:8] = rim_ref[lane, :, at].astype(jnp.float32)
            ext[lane, 8 : 8 + rows] = x_ref[lane, :, at].astype(jnp.float32)
            acc = jnp.zeros((rows, LANES), jnp.float32)
            for j in range(taps):
                acc = acc + w_ref[lane, j : j + 1, at] * ext[lane, 8 - j : 8 - j + rows]
            conv.append(acc)
        q_ref[:, at] = conv[0]
        gated = (conv[1] * conv[2]).astype(jnp.bfloat16).astype(jnp.float32)
        gate[...] = gated
        decay = decay_ref[:, at]
        coef = coef_ref[:, at]
        filt[0:8] = jnp.zeros((8, LANES), jnp.float32)
        for b, part in enumerate(modal_sum(decay, coef, rows, 0.0)):
            filt[8 + 8 * b : 16 + 8 * b] = part.astype(jnp.bfloat16).astype(jnp.float32)
        skip = skip_ref[:, at]
        out = [skip * gated[8 * b : 8 * b + 8] for b in range(nb)]
        for t in range(rows):
            row = jnp.broadcast_to(gate[t : t + 1], (8, LANES))
            for b in range(t // 8, nb):
                start = 8 + 8 * b - t
                out[b] = out[b] + filt[start : start + 8] * row
        for b in range(nb):
            base_ref[8 * b : 8 * b + 8, at] = out[b]
        left = 7.0 - lax.broadcasted_iota(jnp.int32, (8, LANES), 0).astype(jnp.float32)
        ends = []
        for s in range(modes):
            rate = decay[s : s + 1]
            stride = jnp.exp(-8.0 * rate)
            acc = gated[0:8]
            for b in range(1, nb):
                acc = acc * stride + gated[8 * b : 8 * b + 8]
            ends.append(jnp.sum(acc * jnp.exp(-rate * left), axis=0, keepdims=True))
        state_ref[:, at] = jnp.concatenate(ends, axis=0)
        return carry

    lax.fori_loop(0, x_ref.shape[2] // LANES, tile, 0)


def back_kernel(q_ref, base_ref, state_ref, decay_ref, coef_ref, mixed_ref):
    rows = q_ref.shape[0]

    def tile(i, carry):
        at = pl.ds(pl.multiple_of(i * LANES, LANES), LANES)
        far = modal_sum(decay_ref[:, at], coef_ref[:, at] * state_ref[:, at], rows, 1.0)
        whole = jnp.concatenate(far, axis=0) + base_ref[:, at]
        mixed_ref[:, at] = (q_ref[:, at] * whole).astype(jnp.bfloat16)
        return carry

    lax.fori_loop(0, q_ref.shape[1] // LANES, tile, 0)


def per_device(features, short_weight, decay_rate, residue, skip_gain, out_weight):
    lanes, rows, chans = features.shape
    groups, modes = decay_rate.shape
    width = chans // groups
    taps = short_weight.shape[1]
    count = lax.axis_size("ctx")
    tps = lax.axis_size("tp")
    me = lax.axis_index("ctx")
    cb = min(chans, 1024)
    pairs = [(i, i + 1) for i in range(count - 1)]
    rim = lax.ppermute(features[:, rows - (taps - 1) :, :], "ctx", pairs)
    rim = jnp.pad(rim, ((0, 0), (8 - (taps - 1), 0), (0, 0)))
    coef = residue * jnp.sqrt(-jnp.expm1(-2.0 * decay_rate))
    spread = (
        lax.broadcasted_iota(jnp.int32, (groups, chans), 1) // width
        == lax.broadcasted_iota(jnp.int32, (groups, chans), 0)
    ).astype(jnp.float32)
    both = jnp.concatenate([decay_rate, coef], axis=1)
    wide = jnp.einsum("gs,gc->sc", both, spread, precision=lax.Precision.HIGHEST)
    decay_wide, coef_wide = wide[:modes], wide[modes:]
    f32 = jnp.float32
    grid = (chans // cb,)
    plane = pl.BlockSpec((rows, cb), lambda i: (0, i))
    modal = pl.BlockSpec((modes, cb), lambda i: (0, i))
    q, base, own = pl.pallas_call(
        front_kernel,
        grid=grid,
        in_specs=[
            pl.BlockSpec((lanes, rows, cb), lambda i: (0, 0, i)),
            pl.BlockSpec((lanes, 8, cb), lambda i: (0, 0, i)),
            pl.BlockSpec((lanes, taps, cb), lambda i: (0, 0, i)),
            modal,
            modal,
            pl.BlockSpec((1, cb), lambda i: (0, i)),
        ],
        out_specs=[plane, plane, modal],
        out_shape=[
            jax.ShapeDtypeStruct((rows, chans), f32),
            jax.ShapeDtypeStruct((rows, chans), f32),
            jax.ShapeDtypeStruct((modes, chans), f32),
        ],
        scratch_shapes=[
            pltpu.VMEM((lanes, rows + 8, LANES), f32),
            pltpu.VMEM((rows + 8, LANES), f32),
            pltpu.VMEM((rows, LANES), f32),
        ],
        name="front",
    )(features, rim, short_weight, decay_wide, coef_wide, skip_gain[None])
    share = chans // count
    pieces = lax.all_to_all(own, "ctx", split_axis=1, concat_axis=0, tiled=True)
    mine = lax.dynamic_slice_in_dim(decay_wide, me * share, share, axis=1)
    block_decay = jnp.exp(-mine * rows)
    running = jnp.zeros((modes, share), f32)
    before = []
    for b in range(count):
        before.append(running)
        running = running * block_decay + pieces[b * modes : (b + 1) * modes]
    incoming = lax.all_to_all(
        jnp.concatenate(before, axis=0), "ctx", split_axis=0, concat_axis=1, tiled=True
    )
    mixed = pl.pallas_call(
        back_kernel,
        grid=grid,
        in_specs=[plane, plane, modal, modal, modal],
        out_specs=plane,
        out_shape=jax.ShapeDtypeStruct((rows, chans), jnp.bfloat16),
        name="back",
    )(q, base, incoming, decay_wide, coef_wide)
    every = lax.all_gather(mixed, "ctx", axis=0, tiled=True)
    partial_out = jnp.dot(every, out_weight, preferred_element_type=f32)
    cols = out_weight.shape[1]
    sums = lax.psum_scatter(partial_out, "tp", scatter_dimension=1, tiled=True).astype(jnp.bfloat16)
    turned = lax.all_to_all(sums, "ctx", split_axis=0, concat_axis=1, tiled=True)
    part = cols // tps
    swapped = lax.all_to_all(
        turned.reshape(rows, count * part), "tp", split_axis=1, concat_axis=0, tiled=True
    )
    swapped = swapped.reshape(tps, rows, count // tps, part)
    return swapped.transpose(1, 2, 0, 3).reshape(rows, count // tps * cols)


def solution(mesh):
    placed = (
        P(None, "ctx", "tp"),
        P(None, None, "tp"),
        P("tp", None),
        P("tp", None),
        P("tp"),
        P("tp", "ctx"),
    )
    return jax.shard_map(
        per_device, mesh=mesh, in_specs=placed, out_specs=P("ctx", "tp"), check_vma=False
    )
```

time: 833 us -> 222 us (0.27)
  local copies, waits for them, and re-layouts: 454 us -> 6.66 us
  waiting for transfers between devices: 237 us -> 128 us
  matrix products: 75.4 us -> 9.08 us
  Pallas kernels: 0 us -> 14.2 us
    gather x64 -> x0, local copies, waits for them, and re-layouts: 401 us -> none  [near_block(): taps_here[:, clipped]]
    all_gather x2 -> x1, waiting for transfers between devices: 225 us -> 113 us  [per_device(): every = lax.all_gather(mixed, 'ctx', axis=0, tiled=True)]
    dot_general x35 -> x2, matrix products: 75.4 us -> 9.08 us  [the longest x1 6.77 us: per_device(): partial_out = jnp.dot(every, out_weight, preferred_element_type=f32)]
    all_gather x1 -> x0, blocking collectives: 35.3 us -> none  [entering(): pieces = jax.tree.map(lambda part: lax.all_gather(part, axis), value)]
    all_to_all x0 -> x3, blocking collectives: none -> 33.2 us  [the longest x1 15.2 us: per_device(): lax.all_to_all(sums, 'ctx', split_axis=0, concat_axis=1, tiled=True)]
    dynamic_slice x109 -> x0, local copies, waits for them, and re-layouts: 31.2 us -> none  [the longest x45 27.8 us: hop(): longer = join(running, jax.tree.map(lambda part: part[position], pieces))]
    pallas_call x0 -> x2, Pallas kernels: none -> 14.2 us  [the longest x1 9.66 us: per_device(): pl.pallas_call(front_kernel, grid=grid, in_specs=[pl.BlockSpec((lanes, ro...]
  transfers between devices with their start and end apart: 4 -> 4, of which waited for: 2 -> 3; matrix products, arithmetic and copies ran while one was open for 61% -> 2% of each run, Pallas kernels for 0% -> 0%
where the time goes in v1:
time: 222 us; the launch traced here: 221 us
  waiting for transfers between devices  128 us (58%)
  blocking collectives  33.2 us (15%)
  Pallas kernels  14.2 us (6%)
  between operations  13.6 us (6%)
  starting transfers between devices  9.69 us (4%)
  matrix products  9.08 us (4%)
  local copies, waits for them, and re-layouts  6.66 us (3%)
  other arithmetic  5.73 us (3%)
    all_gather x1, waiting for transfers between devices, per_device(): every = lax.all_gather(mixed, 'ctx', axis=0, tiled=True)  113 us
    all_to_all x1, blocking collectives, per_device(): lax.all_to_all(sums, 'ctx', split_axis=0, concat_axis=1, tiled=True)  15.2 us
    all_to_all x1, blocking collectives, per_device(): lax.all_to_all(jnp.concatenate(before, axis=0), 'ctx', split_axis=0, conc...  12.4 us
    pallas_call x1, Pallas kernels, per_device(): pl.pallas_call(front_kernel, grid=grid, in_specs=[pl.BlockSpec((lanes, ro...  9.66 us
    reduce_scatter x1, waiting for transfers between devices, per_device(): lax.psum_scatter(partial_out, 'tp', scatter_dimension=1, tiled=True)  8.02 us
    all_to_all x1, waiting for transfers between devices, per_device(): pieces = lax.all_to_all(own, 'ctx', split_axis=1, concat_axis=0, tiled=True)  7.61 us
    dot_general x1, matrix products, per_device(): partial_out = jnp.dot(every, out_weight, preferred_element_type=f32)  6.77 us
    all_to_all x1, starting transfers between devices, per_device(): pieces = lax.all_to_all(own, 'ctx', split_axis=1, concat_axis=0, tiled=True)  5.66 us
  transfers between devices with their start and end apart: 4, of which 3 were waited for; matrix products, arithmetic and copies ran while one was open for 2% of the time, Pallas kernels for 0%

profile of v1, /device:TPU:1, one launch (start us, length us, event | category | flops | bytes accessed | tf_op | source)
XLA Modules:
  0.0 220.5 jit_solution(11657861342250541462)
XLA Ops:
  6.5 1.1 slice.99
  7.7 3.9 %collective-permute-start = (bf16[3,2,4096]{2,1,0:T(2,128)(2,1)S(1)}, bf16[3,2,4096]{2,1,0:T(2,128)(2,1)S(1)}, u32[]{:S(2)}, u32[]{:S(2)}) collective-permute-start(bf16[3,2,4096]{2,1,0:T(2,128)(2,1)S(1)} %slice.99), channel_id=1, source_target_pairs={{0,2},{2,4},{4,6},{6,8},{8,10},{10,12},{12,14},{14,16},{16,18},{18... | collective-permute-start | bytes 147464 | tf_op jit(solution)/shard_map/ppermute | solution.py:97
  11.7 0.8 sqrt_multiply_fusion
  12.4 2.3 %fusion = f32[32,4096]{1,0:T(8,128)S(1)} fusion(s32[4096]{0:T(1024)S(1)} %get-tuple-element.23, s32[4096]{0:T(1024)S(1)} %get-tuple-element.24, pred[4096]{0:T(1024)(128)(4,1)S(1)} %fusion.24, f32[256,16]{0,1:T(8,128)S(1)} %sqrt_multiply_fusion, f32[256,16]{0,1:T(8,128)} %param.8), kind=kOutput, calls=%fused_computation.1 | convolution fusion | flops 404758528 | bytes 593920 | tf_op jit(solution)/shard_map/gs,gc->sc/dot_general | solution.py:105
  14.7 0.8 fusion.31
  15.6 0.7 pad.4.rim_ref
  16.3 9.7 %front.1 = (f32[64,4096]{1,0:T(8,128)}, f32[64,4096]{1,0:T(8,128)}, f32[16,4096]{1,0:T(8,128)}) custom-call(bf16[3,64,4096]{2,1,0:T(8,128)(2,1)} %x_ref.1, bf16[3,8,4096]{2,1,0:T(8,128)(2,1)} %pad.4.rim_ref, f32[3,3,4096]{2,1,0:T(4,128)} %w_ref.1, f32[16,4096]{1,0:T(8,128)} %get-tuple-element.22.decay_ref, f32[16,4096]{1,0:T(8,128)} %get-tuple-element.21.coef_ref, ...), custom_call_target="tpu_custom_call" | custom-call | tf_op jit(solution)/shard_map/front/pallas_call | solution.py:111
  26.0 1.7 copy.21
  27.7 5.7 %all-to-all-start = ((f32[16,16,256]{2,0,1:T(8,128)}), f32[16,16,256]{2,0,1:T(8,128)S(1)}, u32[]{:S(2)}, u32[]{:S(2)}) async-start(f32[16,16,256]{2,0,1:T(8,128)} %bitcast.143), calls=%async_computation | async-start | bytes 524288 | tf_op jit(solution)/shard_map/all_to_all | solution.py:136
  33.3 0.0 all-gather.2.cloned.1.call-start
  33.4 7.6 %all-to-all-done = f32[16,16,256]{2,0,1:T(8,128)S(1)} async-done(((f32[16,16,256]{2,0,1:T(8,128)}), f32[16,16,256]{2,0,1:T(8,128)S(1)}, u32[]{:S(2)}, u32[]{:S(2)}) %all-to-all-start) | async-done | bytes 262176 | tf_op jit(solution)/shard_map/all_to_all | solution.py:136
  41.0 0.7 constant_dynamic-update-slice_fusion.14
  41.7 0.7 constant_dynamic-update-slice_fusion.13
  42.5 0.7 constant_dynamic-update-slice_fusion.12
  43.2 0.7 constant_dynamic-update-slice_fusion.11
  44.0 0.7 constant_dynamic-update-slice_fusion.10
  45.0 12.4 %all_to_all.67 = f32[16,16,256]{2,1,0:T(8,128)S(1)} all-to-all(f32[16,16,256]{2,1,0:T(8,128)S(1)} %bitcast.166), channel_id=1, replica_groups=mesh['ctx'=16,'tp'=2] {'ctx'}, dimensions={0} | all-to-all | bytes 524288 | tf_op jit(solution)/shard_map/all_to_all | solution.py:144
  57.4 0.7 copy.18
  58.1 4.5 %back.1 = bf16[64,4096]{1,0:T(8,128)(2,1)} custom-call(f32[64,4096]{1,0:T(8,128)} %get-tuple-element.8.q_ref, f32[64,4096]{1,0:T(8,128)} %get-tuple-element.9.base_ref, f32[16,4096]{1,0:T(8,128)} %bitcast.165, f32[16,4096]{1,0:T(8,128)} %get-tuple-element.22.decay_ref, f32[16,4096]{1,0:T(8,128)} %get-tuple-element.21.coef_ref), custom_call_target="tpu_custom_call" | custom-call | tf_op jit(solution)/shard_map/back/pallas_call | solution.py:147
  62.6 0.0 all-gather.2.cloned.1.call-update
  62.6 0.0 reduce-scatter.2.cloned.1.call-start
  62.7 112.8 %all-gather.2.cloned.1.call-done = bf16[1024,4096]{1,0:T(8,128)(2,1)} async-done(((bf16[64,4096]{1,0:T(8,128)(2,1)}), bf16[1024,4096]{1,0:T(8,128)(2,1)}) %all-gather.2.cloned.1.call-update) | async-done | bytes 8388624 | tf_op jit(solution)/shard_map/all_gather | solution.py:155
  175.4 6.8 %fusion.32 = f32[1024,256]{1,0:T(8,128)} fusion(bf16[1024,4096]{1,0:T(8,128)(2,1)} %all-gather.2.cloned.1.call-done, bf16[4096,256]{1,0:T(8,128)(2,1)S(1)} %copy-done), kind=kOutput, calls=%fused_computation.67 | convolution fusion | flops 2147483648 | bytes 11534336 | tf_op jit(solution)/shard_map/dot_general | solution.py:156
  182.2 0.0 reduce-scatter.2.cloned.1.call-update
  182.2 8.0 %reduce-scatter.2.cloned.1.call-done = f32[1024,128]{1,0:T(8,128)} async-done(((f32[1024,256]{1,0:T(8,128)}), f32[1024,128]{1,0:T(8,128)}) %reduce-scatter.2.cloned.1.call-update) | async-done | bytes 524304 | tf_op jit(solution)/shard_map/reduce_scatter | solution.py:158
  190.3 1.1 convert_element_type.6
  191.3 15.2 %all_to_all.68 = bf16[16,64,128]{2,1,0:T(8,128)(2,1)S(1)} all-to-all(bf16[16,64,128]{2,1,0:T(8,128)(2,1)S(1)} %bitcast.160), channel_id=1, replica_groups=mesh['ctx'=16,'tp'=2] {'ctx'}, dimensions={0} | all-to-all | bytes 524288 | tf_op jit(solution)/shard_map/all_to_all | solution.py:159
  206.6 0.2 copy.14
  206.7 0.1 all_to_all.60
  206.9 5.6 %all_to_all.69 = bf16[64,2,1024]{2,0,1:T(8,128)(2,1)S(1)} all-to-all(bf16[64,2,1024]{2,0,1:T(8,128)(2,1)S(1)} %copy.15), channel_id=1, replica_groups=mesh['ctx'=16,'tp'=2] {'tp'}, dimensions={1} | all-to-all | bytes 524288 | tf_op jit(solution)/shard_map/all_to_all | solution.py:161
  212.5 0.3 copy.16
  212.8 0.9 reshape.36
  (21 shorter events, 0.3 us)
Async XLA Ops:
  6.5 168.9 %copy-start = (bf16[4096,256]{1,0:T(8,128)(2,1)S(1)}, bf16[4096,256]{1,0:T(8,128)(2,1)}, u32[]{:S(2)}) copy-start(bf16[4096,256]{1,0:T(8,128)(2,1)} %param.11) | copy-start | bytes 6291460
  7.7 7.9 %collective-permute-start = (bf16[3,2,4096]{2,1,0:T(2,128)(2,1)S(1)}, bf16[3,2,4096]{2,1,0:T(2,128)(2,1)S(1)}, u32[]{:S(2)}, u32[]{:S(2)}) collective-permute-start(bf16[3,2,4096]{2,1,0:T(2,128)(2,1)S(1)} %slice.99), channel_id=1, source_target_pairs={{0,2},{2,4},{4,6},{6,8},{8,10},{10,12},{12,14},{14,16},{16,18},{18... | collective-permute-start | bytes 147464 | tf_op jit(solution)/shard_map/ppermute | solution.py:97
  15.6 29.1 %copy-start.1 = (f32[16,4096]{1,0:T(8,128)S(1)}, f32[16,4096]{1,0:T(8,128)}, u32[]{:S(2)}) copy-start(f32[16,4096]{1,0:T(8,128)} %get-tuple-element.22.decay_ref) | copy-start | bytes 786436
  27.7 13.3 %all-to-all-start = ((f32[16,16,256]{2,0,1:T(8,128)}), f32[16,16,256]{2,0,1:T(8,128)S(1)}, u32[]{:S(2)}, u32[]{:S(2)}) async-start(f32[16,16,256]{2,0,1:T(8,128)} %bitcast.143), calls=%async_computation | async-start | bytes 524288 | tf_op jit(solution)/shard_map/all_to_all | solution.py:136
  33.3 142.1 %all-gather.2.cloned.1.call-start = ((), (), s32[]{:S(2)}) async-start(), calls=%async_computation.5 | async-start | bytes 8912896 | tf_op jit(solution)/shard_map/all_gather | solution.py:155
  62.6 127.6 %reduce-scatter.2.cloned.1.call-start = ((), (), s32[]{:S(2)}) async-start(), calls=%async_computation.6 | async-start | bytes 1572864 | tf_op jit(solution)/shard_map/reduce_scatter | solution.py:158
Sparse Core Ops, SparseCore 0:
  62.8 112.6 all-gather.1
  182.4 7.8 reduce-scatter.1

commit v2 on v1

--- a/solution.py
+++ b/solution.py
@@ -84,6 +84,164 @@
     lax.fori_loop(0, q_ref.shape[1] // LANES, tile, 0)
 
 
+def finish_kernel(
+    q_ref, base_ref, state_ref, decay_ref, coef_ref, own_ref, pair_ref, out_ref,
+    blocks, result, other, packed,
+    up_sem, down_sem, z_sem, ysend_sem, yrecv_sem, psend_sem, precv_sem, osend_sem, orecv_sem,
+):
+    rows = q_ref.shape[0]
+    c, p = lax.axis_index("ctx"), lax.axis_index("tp")
+    x, y, z = c % 2, (c // 2) % 2, c // 4
+    depth = blocks.shape[0] // 2
+    mesh_ids = pl.DeviceIdType.MESH
+    barrier = pltpu.get_barrier_semaphore()
+    for far_z in range(depth):
+        for far_y in range(2):
+            for far_p in range(2):
+                spot = far_z * 4 + far_y * 2 + x
+
+                @pl.when(jnp.logical_or(spot != c, p != far_p))
+                def _():
+                    pl.semaphore_signal(
+                        barrier, inc=1, device_id=(spot, far_p), device_id_type=mesh_ids
+                    )
+
+    here = z * 2 + y
+
+    def tile(i, carry):
+        at = pl.ds(pl.multiple_of(i * LANES, LANES), LANES)
+        far = modal_sum(decay_ref[:, at], coef_ref[:, at] * state_ref[:, at], rows, 1.0)
+        whole = jnp.concatenate(far, axis=0) + base_ref[:, at]
+        blocks[here, :, at] = (q_ref[:, at] * whole).astype(jnp.bfloat16)
+        return carry
+
+    lax.fori_loop(0, q_ref.shape[1] // LANES, tile, 0)
+    pl.semaphore_wait(barrier, depth * 4 - 1)
+
+    def along_z(level, step, sems, k):
+        slot = level * 2 + y
+        return pltpu.make_async_remote_copy(
+            blocks.at[slot], blocks.at[slot], sems.at[k], z_sem.at[level],
+            device_id=(c + 4 * step, p), device_id_type=mesh_ids,
+        )
+
+    def along_y(level):
+        slot = level * 2 + y
+        return pltpu.make_async_remote_copy(
+            blocks.at[slot], blocks.at[slot], ysend_sem.at[level], yrecv_sem.at[level],
+            device_id=(c + 2 - 4 * y, p), device_id_type=mesh_ids,
+        )
+
+    def to_core(level):
+        return pltpu.make_async_remote_copy(
+            result.at[level, 1 - p], other.at[level], psend_sem.at[level], precv_sem.at[level],
+            device_id=(c, 1 - p), device_id_type=mesh_ids,
+        )
+
+    chunk = (c % 8) // 2 * 2 + p
+    side = z // 2
+
+    def to_owner(level, far_y):
+        return pltpu.make_async_remote_copy(
+            packed.at[level, far_y], out_ref.at[chunk], osend_sem.at[level, far_y], orecv_sem.at[chunk],
+            device_id=(level * 4 + far_y * 2 + x, side), device_id_type=mesh_ids,
+        )
+
+    def multiply(level):
+        pltpu.make_async_copy(blocks.at[level * 2 + 1 - y], blocks.at[level * 2 + 1 - y], yrecv_sem.at[level]).wait()
+        lhs = blocks[pl.ds(level * 2, 2)].reshape(2 * rows, blocks.shape[2])
+        result[level, x] = jnp.dot(lhs, own_ref[...], preferred_element_type=jnp.float32)
+        result[level, 1 - x] = jnp.dot(lhs, pair_ref[...], preferred_element_type=jnp.float32)
+        to_core(level).start()
+
+    def deliver(level):
+        to_core(level).wait_recv()
+        total = result[level, p] + other[level]
+        packed[level] = total.astype(jnp.bfloat16).reshape(2, rows, total.shape[1])
+        for far_y in range(2):
+            mine = jnp.logical_and(jnp.logical_and(level == z, far_y == y), side == p)
+
+            @pl.when(mine)
+            def _():
+                out_ref[chunk] = packed[level, far_y]
+
+            @pl.when(jnp.logical_not(mine))
+            def _():
+                to_owner(level, far_y).start()
+
+    def both(k, act):
+        @pl.when(z - k >= 0)
+        def _():
+            act(z - k, 1)
+
+        if k:
+
+            @pl.when(z + k < depth)
+            def _():
+                act(z + k, -1)
+
+    can_up, can_down = z + 1 < depth, z >= 1
+
+    def forward(level, step, k):
+        if k + 1 < depth:
+            if step > 0 or k == 0:
+
+                @pl.when(can_up)
+                def _():
+                    along_z(level, 1, up_sem, k).start()
+
+            if step < 0 or k == 0:
+
+                @pl.when(can_down)
+                def _():
+                    along_z(level, -1, down_sem, k).start()
+
+        along_y(level).start()
+
+    def arrive(k):
+        def act(level, step):
+            pltpu.make_async_copy(blocks.at[level * 2 + y], blocks.at[level * 2 + y], z_sem.at[level]).wait()
+            forward(level, step, k)
+
+        return act
+
+    forward(z, 1, 0)
+    for k in range(1, depth):
+        both(k, arrive(k))
+        both(k - 1, lambda level, step: multiply(level))
+        if k >= 2:
+            both(k - 2, lambda level, step: deliver(level))
+    both(depth - 1, lambda level, step: multiply(level))
+    both(depth - 2, lambda level, step: deliver(level))
+    both(depth - 1, lambda level, step: deliver(level))
+
+    for level in range(depth):
+        along_y(level).wait_send()
+        to_core(level).wait_send()
+        for far_y in range(2):
+            mine = jnp.logical_and(jnp.logical_and(level == z, far_y == y), side == p)
+
+            @pl.when(jnp.logical_not(mine))
+            def _():
+                to_owner(level, far_y).wait_send()
+
+    for k in range(depth - 1):
+
+        @pl.when(jnp.logical_and(z - k >= 0, can_up))
+        def _():
+            along_z(z - k, 1, up_sem, k).wait_send()
+
+        @pl.when(jnp.logical_and(z + k < depth, can_down))
+        def _():
+            along_z(z + k, -1, down_sem, k).wait_send()
+
+    for source in range(out_ref.shape[0]):
+
+        @pl.when(jnp.logical_or(side != p, source != chunk))
+        def _():
+            pltpu.make_async_copy(out_ref.at[source], out_ref.at[source], orecv_sem.at[source]).wait()
+
+
 def per_device(features, short_weight, decay_rate, residue, skip_gain, out_weight):
     lanes, rows, chans = features.shape
     groups, modes = decay_rate.shape
@@ -94,6 +252,8 @@
     me = lax.axis_index("ctx")
     cb = min(chans, 1024)
     pairs = [(i, i + 1) for i in range(count - 1)]
+    if count == 16 and tps == 2:
+        pair_weight = lax.ppermute(out_weight, "ctx", [(i, i ^ 1) for i in range(count)])
     rim = lax.ppermute(features[:, rows - (taps - 1) :, :], "ctx", pairs)
     rim = jnp.pad(rim, ((0, 0), (8 - (taps - 1), 0), (0, 0)))
     coef = residue * jnp.sqrt(-jnp.expm1(-2.0 * decay_rate))
@@ -144,6 +304,40 @@
     incoming = lax.all_to_all(
         jnp.concatenate(before, axis=0), "ctx", split_axis=0, concat_axis=1, tiled=True
     )
+    cols = out_weight.shape[1]
+    if count == 16 and tps == 2:
+        depth = count // 4
+        dma = pltpu.SemaphoreType.DMA
+        vmem = pl.BlockSpec(memory_space=pltpu.VMEM)
+        out = pl.pallas_call(
+            finish_kernel,
+            in_specs=[vmem] * 7,
+            out_specs=vmem,
+            out_shape=jax.ShapeDtypeStruct((count // 2, rows, cols), jnp.bfloat16),
+            scratch_shapes=[
+                pltpu.VMEM((2 * depth, rows, chans), jnp.bfloat16),
+                pltpu.VMEM((depth, 2, 2 * rows, cols), f32),
+                pltpu.VMEM((depth, 2 * rows, cols), f32),
+                pltpu.VMEM((depth, 2, rows, cols), jnp.bfloat16),
+                dma((depth - 1,)),
+                dma((depth - 1,)),
+                dma((depth,)),
+                dma((depth,)),
+                dma((depth,)),
+                dma((depth,)),
+                dma((depth,)),
+                dma((depth, 2)),
+                dma((count // 2,)),
+            ],
+            compiler_params=pltpu.CompilerParams(
+                collective_id=0, has_side_effects=True, vmem_limit_bytes=40 * 1024 * 1024
+            ),
+            cost_estimate=pl.CostEstimate(
+                flops=2 * 8 * rows * chans * 2 * cols, bytes_accessed=8 * 1024 * 1024, transcendentals=0
+            ),
+            name="finish",
+        )(q, base, incoming, decay_wide, coef_wide, out_weight, pair_weight)
+        return out.transpose(1, 0, 2).reshape(rows, count // 2 * cols)
     mixed = pl.pallas_call(
         back_kernel,
         grid=grid,
@@ -154,7 +348,6 @@
     )(q, base, incoming, decay_wide, coef_wide)
     every = lax.all_gather(mixed, "ctx", axis=0, tiled=True)
     partial_out = jnp.dot(every, out_weight, preferred_element_type=f32)
-    cols = out_weight.shape[1]
     sums = lax.psum_scatter(partial_out, "tp", scatter_dimension=1, tiled=True).astype(jnp.bfloat16)
     turned = lax.all_to_all(sums, "ctx", split_axis=0, concat_axis=1, tiled=True)
     part = cols // tps

time: 222 us -> 144 us (0.65)
  waiting for transfers between devices: 128 us -> 6.24 us
  Pallas kernels: 14.2 us -> 73.5 us
  between operations: 13.6 us -> 0.22 us
  blocking collectives: 33.2 us -> 44.1 us
  matrix products: 9.08 us -> 2.31 us
  other arithmetic: 5.73 us -> 1.08 us
    all_gather x1 -> x0, waiting for transfers between devices: 113 us -> none  [per_device(): every = lax.all_gather(mixed, 'ctx', axis=0, tiled=True)]
    pallas_call x1, Pallas kernels: 4.51 us -> 63.9 us  [per_device(): pl.pallas_call(finish_kernel, in_specs=[vmem] * 7, out_specs=vmem, out_sh...]
    all_to_all x1, blocking collectives: 12.4 us -> 44.1 us  [per_device(): lax.all_to_all(jnp.concatenate(before, axis=0), 'ctx', split_axis=0, conc...]
    all_to_all x2 -> x0, blocking collectives: 20.8 us -> none  [the longest x1 15.2 us: per_device(): lax.all_to_all(sums, 'ctx', split_axis=0, concat_axis=1, tiled=True)]
    reduce_scatter x1 -> x0, waiting for transfers between devices: 8.02 us -> none  [per_device(): lax.psum_scatter(partial_out, 'tp', scatter_dimension=1, tiled=True)]
    dot_general x1 -> x0, matrix products: 6.77 us -> none  [per_device(): partial_out = jnp.dot(every, out_weight, preferred_element_type=f32)]
    unnamed x14, other arithmetic: 3.87 us -> 0.29 us
  transfers between devices with their start and end apart: 4 -> 3, of which waited for: 3 -> 1; matrix products, arithmetic and copies ran while one was open for 2% -> 3% of each run, Pallas kernels for 0% -> 0%
where the time goes in v2:
time: 144 us
  Pallas kernels  73.5 us (51%)
  blocking collectives  44.1 us (31%)
  starting transfers between devices  11 us (8%)
  waiting for transfers between devices  6.24 us (4%)
  local copies, waits for them, and re-layouts  5.03 us (3%)
  matrix products  2.31 us (2%)
    pallas_call x1, Pallas kernels, per_device(): pl.pallas_call(finish_kernel, in_specs=[vmem] * 7, out_specs=vmem, out_sh...  63.9 us
    all_to_all x1, blocking collectives, per_device(): lax.all_to_all(jnp.concatenate(before, axis=0), 'ctx', split_axis=0, conc...  44.1 us
    pallas_call x1, Pallas kernels, per_device(): pl.pallas_call(front_kernel, grid=grid, in_specs=[pl.BlockSpec((lanes, ro...  9.66 us
    all_to_all x1, waiting for transfers between devices, per_device(): pieces = lax.all_to_all(own, 'ctx', split_axis=1, concat_axis=0, tiled=True)  6.23 us
    all_to_all x1, starting transfers between devices, per_device(): pieces = lax.all_to_all(own, 'ctx', split_axis=1, concat_axis=0, tiled=True)  5.66 us
    ppermute x1, starting transfers between devices, per_device(): rim = lax.ppermute(features[:, rows - (taps - 1):, :], 'ctx', pairs)  3.95 us
  transfers between devices with their start and end apart: 3, of which 1 were waited for; matrix products, arithmetic and copies ran while one was open for 3% of the time, Pallas kernels for 0%

profile of v2, /device:TPU:1, one launch (start us, length us, event | category | flops | bytes accessed | tf_op | source)
XLA Modules:
  0.0 143.6 jit_solution(2561338028589138589)
XLA Ops:
  0.0 1.0 slice.99
  1.0 3.9 %collective-permute-start = (bf16[3,2,4096]{2,1,0:T(2,128)(2,1)S(1)}, bf16[3,2,4096]{2,1,0:T(2,128)(2,1)S(1)}, u32[]{:S(2)}, u32[]{:S(2)}) collective-permute-start(bf16[3,2,4096]{2,1,0:T(2,128)(2,1)S(1)} %slice.99), channel_id=1, source_target_pairs={{0,2},{2,4},{4,6},{6,8},{8,10},{10,12},{12,14},{14,16},{16,18},{18... | collective-permute-start | bytes 147464 | tf_op jit(solution)/shard_map/ppermute | solution.py:257
  5.0 0.8 sqrt_multiply_fusion
  5.7 2.3 %fusion = f32[32,4096]{1,0:T(8,128)S(1)} fusion(s32[4096]{0:T(1024)S(1)} %get-tuple-element.23, s32[4096]{0:T(1024)S(1)} %get-tuple-element.24, pred[4096]{0:T(1024)(128)(4,1)S(1)} %fusion.24, f32[256,16]{0,1:T(8,128)S(1)} %sqrt_multiply_fusion, f32[256,16]{0,1:T(8,128)} %param.8), kind=kOutput, calls=%fused_computation.1 | convolution fusion | flops 404758528 | bytes 593920 | tf_op jit(solution)/shard_map/gs,gc->sc/dot_general | solution.py:265
  8.0 0.8 fusion.31
  8.9 0.0 copy-start.2
  8.9 0.0 copy-start
  8.9 0.0 collective-permute-done
  8.9 0.7 pad.4.rim_ref
  9.6 9.7 %front.1 = (f32[64,4096]{1,0:T(8,128)}, f32[64,4096]{1,0:T(8,128)}, f32[16,4096]{1,0:T(8,128)}) custom-call(bf16[3,64,4096]{2,1,0:T(8,128)(2,1)} %x_ref.1, bf16[3,8,4096]{2,1,0:T(8,128)(2,1)} %pad.4.rim_ref, f32[3,3,4096]{2,1,0:T(4,128)} %w_ref.1, f32[16,4096]{1,0:T(8,128)} %get-tuple-element.22.decay_ref, f32[16,4096]{1,0:T(8,128)} %get-tuple-element.21.coef_ref, ...), custom_call_target="tpu_custom_call" | custom-call | tf_op jit(solution)/shard_map/front/pallas_call | solution.py:271
  19.3 0.0 copy-start.1
  19.3 1.7 %copy.15 = f32[2,16,8,256]{3,2,0,1:T(8,128)} copy(f32[2,16,8,256]{3,2,1,0:T(8,128)} %bitcast.154) | data formatting | bytes 524288 | tf_op jit(solution)/shard_map/all_to_all | solution.py:296
  21.0 5.7 %all-to-all-start = ((f32[16,16,256]{2,0,1:T(8,128)}), f32[16,16,256]{2,0,1:T(8,128)S(1)}, u32[]{:S(2)}, u32[]{:S(2)}) async-start(f32[16,16,256]{2,0,1:T(8,128)} %bitcast.134), calls=%async_computation | async-start | bytes 524288 | tf_op jit(solution)/shard_map/all_to_all | solution.py:296
  26.7 0.0 copy-done.2
  26.7 1.4 collective-permute-start.1
  28.1 6.2 %all-to-all-done = f32[16,16,256]{2,0,1:T(8,128)S(1)} async-done(((f32[16,16,256]{2,0,1:T(8,128)}), f32[16,16,256]{2,0,1:T(8,128)S(1)}, u32[]{:S(2)}, u32[]{:S(2)}) %all-to-all-start) | async-done | bytes 262176 | tf_op jit(solution)/shard_map/all_to_all | solution.py:296
  34.3 0.0 copy-start.3
  34.3 0.0 copy-start.4
  34.3 0.0 copy-done
  34.8 44.1 %all_to_all.35 = f32[16,16,256]{2,1,0:T(8,128)S(1)} all-to-all(f32[16,16,256]{2,1,0:T(8,128)S(1)} %bitcast.153), channel_id=1, replica_groups=mesh['ctx'=16,'tp'=2] {'ctx'}, dimensions={0} | all-to-all | bytes 524288 | tf_op jit(solution)/shard_map/all_to_all | solution.py:304
  78.9 0.0 collective-permute-done.1.pair_ref
  78.9 0.0 copy-done.1
  78.9 0.0 copy-done.3
  78.9 0.0 copy-done.4
  78.9 63.9 %finish.1 = bf16[8,64,256]{2,1,0:T(8,128)(2,1)S(1)} custom-call(f32[64,4096]{1,0:T(8,128)S(1)} %copy-done.3, f32[64,4096]{1,0:T(8,128)S(1)} %copy-done.4, f32[16,4096]{1,0:T(8,128)S(1)} %bitcast.135, f32[16,4096]{1,0:T(8,128)S(1)} %copy-done, f32[16,4096]{1,0:T(8,128)S(1)} %copy-done.1, bf16[4096,256]{1,0:T(8,128)(2,1)S(1)} %copy-done.2, ...), custom_call_target="tpu_custom_call" | custom-call | flops 2147483648 | bytes 8388608 | tf_op jit(solution)/shard_map/finish/pallas_call | solution.py:312
  142.8 0.7 copy.13
  (19 shorter events, 0.3 us)
Async XLA Ops:
  1.0 7.9 %collective-permute-start = (bf16[3,2,4096]{2,1,0:T(2,128)(2,1)S(1)}, bf16[3,2,4096]{2,1,0:T(2,128)(2,1)S(1)}, u32[]{:S(2)}, u32[]{:S(2)}) collective-permute-start(bf16[3,2,4096]{2,1,0:T(2,128)(2,1)S(1)} %slice.99), channel_id=1, source_target_pairs={{0,2},{2,4},{4,6},{6,8},{8,10},{10,12},{12,14},{14,16},{16,18},{18... | collective-permute-start | bytes 147464 | tf_op jit(solution)/shard_map/ppermute | solution.py:257
  8.9 17.8 %copy-start.2 = (bf16[4096,256]{1,0:T(8,128)(2,1)S(1)}, bf16[4096,256]{1,0:T(8,128)(2,1)}, u32[]{:S(2)}) copy-start(bf16[4096,256]{1,0:T(8,128)(2,1)} %own_ref.1) | copy-start | bytes 6291460
  8.9 25.5 %copy-start = (f32[16,4096]{1,0:T(8,128)S(1)}, f32[16,4096]{1,0:T(8,128)}, u32[]{:S(2)}) copy-start(f32[16,4096]{1,0:T(8,128)} %get-tuple-element.22.decay_ref) | copy-start | bytes 786436
  19.3 59.6 %copy-start.1 = (f32[16,4096]{1,0:T(8,128)S(1)}, f32[16,4096]{1,0:T(8,128)}, u32[]{:S(2)}) copy-start(f32[16,4096]{1,0:T(8,128)} %get-tuple-element.21.coef_ref) | copy-start | bytes 786436
  21.0 13.3 %all-to-all-start = ((f32[16,16,256]{2,0,1:T(8,128)}), f32[16,16,256]{2,0,1:T(8,128)S(1)}, u32[]{:S(2)}, u32[]{:S(2)}) async-start(f32[16,16,256]{2,0,1:T(8,128)} %bitcast.134), calls=%async_computation | async-start | bytes 524288 | tf_op jit(solution)/shard_map/all_to_all | solution.py:296
  26.7 52.2 %collective-permute-start.1 = (bf16[4096,256]{1,0:T(8,128)(2,1)S(1)}, bf16[4096,256]{1,0:T(8,128)(2,1)}, u32[]{:S(2)}, u32[]{:S(2)}) collective-permute-start(bf16[4096,256]{1,0:T(8,128)(2,1)S(1)} %copy-done.2), channel_id=1, source_target_pairs={{0,2},{2,0},{4,6},{6,4},{8,10},{10,8},{12,14},{14,12},{16,18},{18,... | collective-permute-start | bytes 6291464 | tf_op jit(solution)/shard_map/ppermute | solution.py:256
  34.3 44.6 %copy-start.3 = (f32[64,4096]{1,0:T(8,128)S(1)}, f32[64,4096]{1,0:T(8,128)}, u32[]{:S(2)}) copy-start(f32[64,4096]{1,0:T(8,128)} %get-tuple-element.8.q_ref) | copy-start | bytes 3145732
  34.3 44.6 %copy-start.4 = (f32[64,4096]{1,0:T(8,128)S(1)}, f32[64,4096]{1,0:T(8,128)}, u32[]{:S(2)}) copy-start(f32[64,4096]{1,0:T(8,128)} %get-tuple-element.9.base_ref) | copy-start | bytes 3145732

commit v3 on v2

--- a/solution.py
+++ b/solution.py
@@ -6,6 +6,7 @@
 from jax.sharding import PartitionSpec as P
 
 LANES = 128
+WCUTS = 4
 
 
 def modal_sum(decay, weight, rows, shift):
@@ -85,8 +86,8 @@
 
 
 def finish_kernel(
-    q_ref, base_ref, state_ref, decay_ref, coef_ref, own_ref, pair_ref, out_ref,
-    blocks, result, other, packed,
+    q_ref, base_ref, state_ref, decay_ref, coef_ref, own_ref, out_ref,
+    blocks, result, other, packed, pair, wsend_sem, wrecv_sem,
     up_sem, down_sem, z_sem, ysend_sem, yrecv_sem, psend_sem, precv_sem, osend_sem, orecv_sem,
 ):
     rows = q_ref.shape[0]
@@ -106,7 +107,17 @@
                         barrier, inc=1, device_id=(spot, far_p), device_id_type=mesh_ids
                     )
 
+    beside = c + 1 - 2 * x
+    pl.semaphore_signal(barrier, inc=1, device_id=(beside, p), device_id_type=mesh_ids)
     here = z * 2 + y
+    span = own_ref.shape[0] // WCUTS
+
+    def weights(k):
+        at = pl.ds(k * span, span)
+        return pltpu.make_async_remote_copy(
+            own_ref.at[at], pair.at[at], wsend_sem.at[k], wrecv_sem.at[k],
+            device_id=(beside, p), device_id_type=mesh_ids,
+        )
 
     def tile(i, carry):
         at = pl.ds(pl.multiple_of(i * LANES, LANES), LANES)
@@ -116,7 +127,7 @@
         return carry
 
     lax.fori_loop(0, q_ref.shape[1] // LANES, tile, 0)
-    pl.semaphore_wait(barrier, depth * 4 - 1)
+    pl.semaphore_wait(barrier, depth * 4)
 
     def along_z(level, step, sems, k):
         slot = level * 2 + y
@@ -151,8 +162,6 @@
         pltpu.make_async_copy(blocks.at[level * 2 + 1 - y], blocks.at[level * 2 + 1 - y], yrecv_sem.at[level]).wait()
         lhs = blocks[pl.ds(level * 2, 2)].reshape(2 * rows, blocks.shape[2])
         result[level, x] = jnp.dot(lhs, own_ref[...], preferred_element_type=jnp.float32)
-        result[level, 1 - x] = jnp.dot(lhs, pair_ref[...], preferred_element_type=jnp.float32)
-        to_core(level).start()
 
     def deliver(level):
         to_core(level).wait_recv()
@@ -206,14 +215,22 @@
         return act
 
     forward(z, 1, 0)
+    for k in range(WCUTS):
+        weights(k).start()
     for k in range(1, depth):
         both(k, arrive(k))
         both(k - 1, lambda level, step: multiply(level))
-        if k >= 2:
-            both(k - 2, lambda level, step: deliver(level))
     both(depth - 1, lambda level, step: multiply(level))
-    both(depth - 2, lambda level, step: deliver(level))
-    both(depth - 1, lambda level, step: deliver(level))
+    for k in range(WCUTS):
+        weights(k).wait()
+        lhs = blocks[:, :, k * span : (k + 1) * span].reshape(2 * depth * rows, span)
+        term = jnp.dot(lhs, pair[k * span : (k + 1) * span], preferred_element_type=jnp.float32)
+        term = term.reshape(depth, 2 * rows, term.shape[1])
+        result[:, 1 - x] = term if k == 0 else result[:, 1 - x] + term
+    for level in range(depth):
+        to_core(level).start()
+    for level in range(depth):
+        deliver(level)
 
     for level in range(depth):
         along_y(level).wait_send()
@@ -252,8 +269,6 @@
     me = lax.axis_index("ctx")
     cb = min(chans, 1024)
     pairs = [(i, i + 1) for i in range(count - 1)]
-    if count == 16 and tps == 2:
-        pair_weight = lax.ppermute(out_weight, "ctx", [(i, i ^ 1) for i in range(count)])
     rim = lax.ppermute(features[:, rows - (taps - 1) :, :], "ctx", pairs)
     rim = jnp.pad(rim, ((0, 0), (8 - (taps - 1), 0), (0, 0)))
     coef = residue * jnp.sqrt(-jnp.expm1(-2.0 * decay_rate))
@@ -311,7 +326,7 @@
         vmem = pl.BlockSpec(memory_space=pltpu.VMEM)
         out = pl.pallas_call(
             finish_kernel,
-            in_specs=[vmem] * 7,
+            in_specs=[vmem] * 6,
             out_specs=vmem,
             out_shape=jax.ShapeDtypeStruct((count // 2, rows, cols), jnp.bfloat16),
             scratch_shapes=[
@@ -319,6 +334,9 @@
                 pltpu.VMEM((depth, 2, 2 * rows, cols), f32),
                 pltpu.VMEM((depth, 2 * rows, cols), f32),
                 pltpu.VMEM((depth, 2, rows, cols), jnp.bfloat16),
+                pltpu.VMEM(out_weight.shape, jnp.bfloat16),
+                dma((WCUTS,)),
+                dma((WCUTS,)),
                 dma((depth - 1,)),
                 dma((depth - 1,)),
                 dma((depth,)),
@@ -336,7 +354,7 @@
                 flops=2 * 8 * rows * chans * 2 * cols, bytes_accessed=8 * 1024 * 1024, transcendentals=0
             ),
             name="finish",
-        )(q, base, incoming, decay_wide, coef_wide, out_weight, pair_weight)
+        )(q, base, incoming, decay_wide, coef_wide, out_weight)
         return out.transpose(1, 0, 2).reshape(rows, count // 2 * cols)
     mixed = pl.pallas_call(
         back_kernel,

time: 144 us -> 115 us (0.80)
  blocking collectives: 44.1 us -> 12.4 us
  local copies, waits for them, and re-layouts: 5.03 us -> 7.59 us
    all_to_all x1, blocking collectives: 44.1 us -> 12.4 us  [per_device(): lax.all_to_all(jnp.concatenate(before, axis=0), 'ctx', split_axis=0, conc...]
    unnamed x11, local copies, waits for them, and re-layouts: 0.02 us -> 2.46 us
  transfers between devices with their start and end apart: 3 -> 2, of which waited for: 1 -> 1; matrix products, arithmetic and copies ran while one was open for 3% -> 3% of each run, Pallas kernels for 0% -> 0%
where the time goes in v3:
time: 115 us; the launch traced here: 114 us
  Pallas kernels  73.3 us (64%)
  blocking collectives  12.4 us (11%)
  starting transfers between devices  9.61 us (8%)
  waiting for transfers between devices  7.66 us (7%)
  local copies, waits for them, and re-layouts  7.59 us (7%)
  matrix products  2.31 us (2%)
    pallas_call x1, Pallas kernels, per_device(): pl.pallas_call(finish_kernel, in_specs=[vmem] * 6, out_specs=vmem, out_sh...  63.7 us
    all_to_all x1, blocking collectives, per_device(): lax.all_to_all(jnp.concatenate(before, axis=0), 'ctx', split_axis=0, conc...  12.4 us
    pallas_call x1, Pallas kernels, per_device(): pl.pallas_call(front_kernel, grid=grid, in_specs=[pl.BlockSpec((lanes, ro...  9.58 us
    all_to_all x1, waiting for transfers between devices, per_device(): pieces = lax.all_to_all(own, 'ctx', split_axis=1, concat_axis=0, tiled=True)  7.66 us
    all_to_all x1, starting transfers between devices, per_device(): pieces = lax.all_to_all(own, 'ctx', split_axis=1, concat_axis=0, tiled=True)  5.66 us
    ppermute x1, starting transfers between devices, per_device(): rim = lax.ppermute(features[:, rows - (taps - 1):, :], 'ctx', pairs)  3.95 us
    unnamed x11, local copies, waits for them, and re-layouts  2.46 us
    dot_general x1, matrix products, per_device(): jnp.einsum('gs,gc->sc', both, spread, precision=lax.Precision.HIGHEST)  2.31 us
  transfers between devices with their start and end apart: 2, of which 1 were waited for; matrix products, arithmetic and copies ran while one was open for 3% of the time, Pallas kernels for 0%

profile of v3, /device:TPU:1, one launch (start us, length us, event | category | flops | bytes accessed | tf_op | source)
XLA Modules:
  0.0 114.2 jit_solution(2919369266042520487)
XLA Ops:
  0.0 1.0 slice.99
  1.0 3.9 %collective-permute-start = (bf16[3,2,4096]{2,1,0:T(2,128)(2,1)S(1)}, bf16[3,2,4096]{2,1,0:T(2,128)(2,1)S(1)}, u32[]{:S(2)}, u32[]{:S(2)}) collective-permute-start(bf16[3,2,4096]{2,1,0:T(2,128)(2,1)S(1)} %slice.99), channel_id=1, source_target_pairs={{0,2},{2,4},{4,6},{6,8},{8,10},{10,12},{12,14},{14,16},{16,18},{18... | collective-permute-start | bytes 147464 | tf_op jit(solution)/shard_map/ppermute | solution.py:272
  5.0 0.8 sqrt_multiply_fusion
  5.7 2.3 %fusion = f32[32,4096]{1,0:T(8,128)S(1)} fusion(s32[4096]{0:T(1024)S(1)} %get-tuple-element.23, s32[4096]{0:T(1024)S(1)} %get-tuple-element.24, pred[4096]{0:T(1024)(128)(4,1)S(1)} %fusion.24, f32[256,16]{0,1:T(8,128)S(1)} %sqrt_multiply_fusion, f32[256,16]{0,1:T(8,128)} %param.8), kind=kOutput, calls=%fused_computation.1 | convolution fusion | flops 404758528 | bytes 593920 | tf_op jit(solution)/shard_map/gs,gc->sc/dot_general | solution.py:280
  8.0 0.8 fusion.31
  8.9 0.0 copy-start
  8.9 0.0 collective-permute-done
  8.9 0.7 pad.4.rim_ref
  9.6 9.6 %front.1 = (f32[64,4096]{1,0:T(8,128)}, f32[64,4096]{1,0:T(8,128)}, f32[16,4096]{1,0:T(8,128)}) custom-call(bf16[3,64,4096]{2,1,0:T(8,128)(2,1)} %x_ref.1, bf16[3,8,4096]{2,1,0:T(8,128)(2,1)} %pad.4.rim_ref, f32[3,3,4096]{2,1,0:T(4,128)} %w_ref.1, f32[16,4096]{1,0:T(8,128)} %get-tuple-element.22.decay_ref, f32[16,4096]{1,0:T(8,128)} %get-tuple-element.21.coef_ref, ...), custom_call_target="tpu_custom_call" | custom-call | tf_op jit(solution)/shard_map/front/pallas_call | solution.py:286
  19.2 0.0 copy-start.1
  19.2 0.0 copy-start.2
  19.2 1.8 %copy.15 = f32[2,16,8,256]{3,2,0,1:T(8,128)} copy(f32[2,16,8,256]{3,2,1,0:T(8,128)} %bitcast.154) | data formatting | bytes 524288 | tf_op jit(solution)/shard_map/all_to_all | solution.py:311
  21.1 5.7 %all-to-all-start = ((f32[16,16,256]{2,0,1:T(8,128)}), f32[16,16,256]{2,0,1:T(8,128)S(1)}, u32[]{:S(2)}, u32[]{:S(2)}) async-start(f32[16,16,256]{2,0,1:T(8,128)} %bitcast.134), calls=%async_computation | async-start | bytes 524288 | tf_op jit(solution)/shard_map/all_to_all | solution.py:311
  26.7 7.7 %all-to-all-done = f32[16,16,256]{2,0,1:T(8,128)S(1)} async-done(((f32[16,16,256]{2,0,1:T(8,128)}), f32[16,16,256]{2,0,1:T(8,128)S(1)}, u32[]{:S(2)}, u32[]{:S(2)}) %all-to-all-start) | async-done | bytes 262176 | tf_op jit(solution)/shard_map/all_to_all | solution.py:311
  34.4 0.0 copy-done
  34.8 12.4 %all_to_all.35 = f32[16,16,256]{2,1,0:T(8,128)S(1)} all-to-all(f32[16,16,256]{2,1,0:T(8,128)S(1)} %bitcast.153), channel_id=1, replica_groups=mesh['ctx'=16,'tp'=2] {'ctx'}, dimensions={0} | all-to-all | bytes 524288 | tf_op jit(solution)/shard_map/all_to_all | solution.py:319
  47.2 0.0 copy-done.1
  47.2 0.0 copy-done.2
  47.2 0.0 copy-start.3
  47.2 1.2 %copy-done.3 = f32[64,4096]{1,0:T(8,128)S(1)} copy-done((f32[64,4096]{1,0:T(8,128)S(1)}, f32[64,4096]{1,0:T(8,128)}, u32[]{:S(2)}) %copy-start.3) | copy-done | bytes 1048600
  48.5 0.0 copy-start.4
  48.5 1.2 %copy-done.4 = f32[64,4096]{1,0:T(8,128)S(1)} copy-done((f32[64,4096]{1,0:T(8,128)S(1)}, f32[64,4096]{1,0:T(8,128)}, u32[]{:S(2)}) %copy-start.4) | copy-done | bytes 1048600
  49.7 63.7 %finish.1 = bf16[8,64,256]{2,1,0:T(8,128)(2,1)S(1)} custom-call(f32[64,4096]{1,0:T(8,128)S(1)} %copy-done.3, f32[64,4096]{1,0:T(8,128)S(1)} %copy-done.4, f32[16,4096]{1,0:T(8,128)S(1)} %bitcast.135, f32[16,4096]{1,0:T(8,128)S(1)} %copy-done, f32[16,4096]{1,0:T(8,128)S(1)} %copy-done.1, bf16[4096,256]{1,0:T(8,128)(2,1)S(1)} %copy-done.2), custom_call_target="tpu_custom_call" | custom-call | flops 2147483648 | bytes 8388608 | tf_op jit(solution)/shard_map/finish/pallas_call | solution.py:327
  113.4 0.7 copy.13
  (19 shorter events, 0.3 us)
Async XLA Ops:
  1.0 7.9 %collective-permute-start = (bf16[3,2,4096]{2,1,0:T(2,128)(2,1)S(1)}, bf16[3,2,4096]{2,1,0:T(2,128)(2,1)S(1)}, u32[]{:S(2)}, u32[]{:S(2)}) collective-permute-start(bf16[3,2,4096]{2,1,0:T(2,128)(2,1)S(1)} %slice.99), channel_id=1, source_target_pairs={{0,2},{2,4},{4,6},{6,8},{8,10},{10,12},{12,14},{14,16},{16,18},{18... | collective-permute-start | bytes 147464 | tf_op jit(solution)/shard_map/ppermute | solution.py:272
  8.9 25.5 %copy-start = (f32[16,4096]{1,0:T(8,128)S(1)}, f32[16,4096]{1,0:T(8,128)}, u32[]{:S(2)}) copy-start(f32[16,4096]{1,0:T(8,128)} %get-tuple-element.22.decay_ref) | copy-start | bytes 786436
  19.2 28.0 %copy-start.1 = (f32[16,4096]{1,0:T(8,128)S(1)}, f32[16,4096]{1,0:T(8,128)}, u32[]{:S(2)}) copy-start(f32[16,4096]{1,0:T(8,128)} %get-tuple-element.21.coef_ref) | copy-start | bytes 786436
  19.2 28.0 %copy-start.2 = (bf16[4096,256]{1,0:T(8,128)(2,1)S(1)}, bf16[4096,256]{1,0:T(8,128)(2,1)}, u32[]{:S(2)}) copy-start(bf16[4096,256]{1,0:T(8,128)(2,1)} %own_ref.1) | copy-start | bytes 6291460
  21.1 13.3 %all-to-all-start = ((f32[16,16,256]{2,0,1:T(8,128)}), f32[16,16,256]{2,0,1:T(8,128)S(1)}, u32[]{:S(2)}, u32[]{:S(2)}) async-start(f32[16,16,256]{2,0,1:T(8,128)} %bitcast.134), calls=%async_computation | async-start | bytes 524288 | tf_op jit(solution)/shard_map/all_to_all | solution.py:311
  47.2 1.2 %copy-start.3 = (f32[64,4096]{1,0:T(8,128)S(1)}, f32[64,4096]{1,0:T(8,128)}, u32[]{:S(2)}) copy-start(f32[64,4096]{1,0:T(8,128)} %get-tuple-element.8.q_ref) | copy-start | bytes 3145732
  48.5 1.2 %copy-start.4 = (f32[64,4096]{1,0:T(8,128)S(1)}, f32[64,4096]{1,0:T(8,128)}, u32[]{:S(2)}) copy-start(f32[64,4096]{1,0:T(8,128)} %get-tuple-element.9.base_ref) | copy-start | bytes 3145732

commit v4 on v3

--- a/solution.py
+++ b/solution.py
@@ -24,49 +24,55 @@
     return total
 
 
-def front_kernel(x_ref, rim_ref, w_ref, decay_ref, coef_ref, skip_ref, q_ref, base_ref, state_ref, ext, filt, gate):
+def front_tile(at, x_ref, rim_ref, w_ref, decay_ref, coef_ref, skip_ref, q_ref, base_ref, ext, filt, gate):
     rows = x_ref.shape[1]
     taps = w_ref.shape[1]
     modes = decay_ref.shape[0]
     nb = rows // 8
 
+    conv = []
+    for lane in range(3):
+        ext[lane, 0:8] = rim_ref[lane, :, at].astype(jnp.float32)
+        ext[lane, 8 : 8 + rows] = x_ref[lane, :, at].astype(jnp.float32)
+        acc = jnp.zeros((rows, LANES), jnp.float32)
+        for j in range(taps):
+            acc = acc + w_ref[lane, j : j + 1, at] * ext[lane, 8 - j : 8 - j + rows]
+        conv.append(acc)
+    q_ref[:, at] = conv[0]
+    gated = (conv[1] * conv[2]).astype(jnp.bfloat16).astype(jnp.float32)
+    gate[...] = gated
+    decay = decay_ref[:, at]
+    coef = coef_ref[:, at]
+    filt[0:8] = jnp.zeros((8, LANES), jnp.float32)
+    for b, part in enumerate(modal_sum(decay, coef, rows, 0.0)):
+        filt[8 + 8 * b : 16 + 8 * b] = part.astype(jnp.bfloat16).astype(jnp.float32)
+    skip = skip_ref[:, at]
+    out = [skip * gated[8 * b : 8 * b + 8] for b in range(nb)]
+    for t in range(rows):
+        row = jnp.broadcast_to(gate[t : t + 1], (8, LANES))
+        for b in range(t // 8, nb):
+            start = 8 + 8 * b - t
+            out[b] = out[b] + filt[start : start + 8] * row
+    for b in range(nb):
+        base_ref[8 * b : 8 * b + 8, at] = out[b]
+    left = 7.0 - lax.broadcasted_iota(jnp.int32, (8, LANES), 0).astype(jnp.float32)
+    ends = []
+    for s in range(modes):
+        rate = decay[s : s + 1]
+        stride = jnp.exp(-8.0 * rate)
+        acc = gated[0:8]
+        for b in range(1, nb):
+            acc = acc * stride + gated[8 * b : 8 * b + 8]
+        ends.append(jnp.sum(acc * jnp.exp(-rate * left), axis=0, keepdims=True))
+    return jnp.concatenate(ends, axis=0)
+
+
+def front_kernel(x_ref, rim_ref, w_ref, decay_ref, coef_ref, skip_ref, q_ref, base_ref, state_ref, ext, filt, gate):
     def tile(i, carry):
         at = pl.ds(pl.multiple_of(i * LANES, LANES), LANES)
-        conv = []
-        for lane in range(3):
-            ext[lane, 0:8] = rim_ref[lane, :, at].astype(jnp.float32)
-            ext[lane, 8 : 8 + rows] = x_ref[lane, :, at].astype(jnp.float32)
-            acc = jnp.zeros((rows, LANES), jnp.float32)
-            for j in range(taps):
-                acc = acc + w_ref[lane, j : j + 1, at] * ext[lane, 8 - j : 8 - j + rows]
-            conv.append(acc)
-        q_ref[:, at] = conv[0]
-        gated = (conv[1] * conv[2]).astype(jnp.bfloat16).astype(jnp.float32)
-        gate[...] = gated
-        decay = decay_ref[:, at]
-        coef = coef_ref[:, at]
-        filt[0:8] = jnp.zeros((8, LANES), jnp.float32)
-        for b, part in enumerate(modal_sum(decay, coef, rows, 0.0)):
-            filt[8 + 8 * b : 16 + 8 * b] = part.astype(jnp.bfloat16).astype(jnp.float32)
-        skip = skip_ref[:, at]
-        out = [skip * gated[8 * b : 8 * b + 8] for b in range(nb)]
-        for t in range(rows):
-            row = jnp.broadcast_to(gate[t : t + 1], (8, LANES))
-            for b in range(t // 8, nb):
-                start = 8 + 8 * b - t
-                out[b] = out[b] + filt[start : start + 8] * row
-        for b in range(nb):
-            base_ref[8 * b : 8 * b + 8, at] = out[b]
-        left = 7.0 - lax.broadcasted_iota(jnp.int32, (8, LANES), 0).astype(jnp.float32)
-        ends = []
-        for s in range(modes):
-            rate = decay[s : s + 1]
-            stride = jnp.exp(-8.0 * rate)
-            acc = gated[0:8]
-            for b in range(1, nb):
-                acc = acc * stride + gated[8 * b : 8 * b + 8]
-            ends.append(jnp.sum(acc * jnp.exp(-rate * left), axis=0, keepdims=True))
-        state_ref[:, at] = jnp.concatenate(ends, axis=0)
+        state_ref[:, at] = front_tile(
+            at, x_ref, rim_ref, w_ref, decay_ref, coef_ref, skip_ref, q_ref, base_ref, ext, filt, gate
+        )
         return carry
 
     lax.fori_loop(0, x_ref.shape[2] // LANES, tile, 0)
@@ -86,29 +92,29 @@
 
 
 def finish_kernel(
-    q_ref, base_ref, state_ref, decay_ref, coef_ref, own_ref, out_ref,
+    x_ref, rim_ref, w_ref, decay_ref, coef_ref, skip_ref, own_ref, out_ref,
+    q_ref, base_ref, ext, filt, gate, ends, gathered, ready, incoming,
+    send1_sem, recv1_sem, send2_sem, recv2_sem,
     blocks, result, other, packed, pair, wsend_sem, wrecv_sem,
     up_sem, down_sem, z_sem, ysend_sem, yrecv_sem, psend_sem, precv_sem, osend_sem, orecv_sem,
 ):
     rows = q_ref.shape[0]
+    count, modes, share = ends.shape
     c, p = lax.axis_index("ctx"), lax.axis_index("tp")
     x, y, z = c % 2, (c // 2) % 2, c // 4
     depth = blocks.shape[0] // 2
     mesh_ids = pl.DeviceIdType.MESH
     barrier = pltpu.get_barrier_semaphore()
-    for far_z in range(depth):
-        for far_y in range(2):
-            for far_p in range(2):
-                spot = far_z * 4 + far_y * 2 + x
-
-                @pl.when(jnp.logical_or(spot != c, p != far_p))
-                def _():
-                    pl.semaphore_signal(
-                        barrier, inc=1, device_id=(spot, far_p), device_id_type=mesh_ids
-                    )
-
+    for spot in range(count):
+
+        @pl.when(spot != c)
+        def _():
+            pl.semaphore_signal(barrier, inc=1, device_id=(spot, p), device_id_type=mesh_ids)
+
+    for far in range(2 * depth):
+        pl.semaphore_signal(barrier, inc=1, device_id=(far * 2 + x, 1 - p), device_id_type=mesh_ids)
+    pl.semaphore_wait(barrier, count - 1 + 2 * depth)
     beside = c + 1 - 2 * x
-    pl.semaphore_signal(barrier, inc=1, device_id=(beside, p), device_id_type=mesh_ids)
     here = z * 2 + y
     span = own_ref.shape[0] // WCUTS
 
@@ -119,15 +125,73 @@
             device_id=(beside, p), device_id_type=mesh_ids,
         )
 
-    def tile(i, carry):
-        at = pl.ds(pl.multiple_of(i * LANES, LANES), LANES)
-        far = modal_sum(decay_ref[:, at], coef_ref[:, at] * state_ref[:, at], rows, 1.0)
-        whole = jnp.concatenate(far, axis=0) + base_ref[:, at]
-        blocks[here, :, at] = (q_ref[:, at] * whole).astype(jnp.bfloat16)
+    halves = share // LANES
+
+    def hand_over(d):
+        return pltpu.make_async_remote_copy(
+            ends.at[d], gathered.at[c], send1_sem.at[d], recv1_sem.at[c],
+            device_id=(d, p), device_id_type=mesh_ids,
+        )
+
+    def hand_back(d):
+        return pltpu.make_async_remote_copy(
+            ready.at[d], incoming.at[c], send2_sem.at[d], recv2_sem.at[c],
+            device_id=(d, p), device_id_type=mesh_ids,
+        )
+
+    def landed(buf, sems, d):
+        pltpu.make_async_copy(buf.at[d], buf.at[d], sems.at[d]).wait()
+
+    def front_step(j, carry):
+        d = lax.rem(c + 1 + j, count)
+        for h in range(halves):
+            at = pl.ds(pl.multiple_of(d * share + h * LANES, LANES), LANES)
+            ends[d, :, h * LANES : (h + 1) * LANES] = front_tile(
+                at, x_ref, rim_ref, w_ref, decay_ref, coef_ref, skip_ref, q_ref, base_ref, ext, filt, gate
+            )
+
+        @pl.when(d != c)
+        def _():
+            hand_over(d).start()
+
         return carry
 
-    lax.fori_loop(0, q_ref.shape[1] // LANES, tile, 0)
-    pl.semaphore_wait(barrier, depth * 4)
+    lax.fori_loop(0, count, front_step, 0)
+    gathered[c] = ends[c]
+    mine = decay_ref[:, pl.ds(pl.multiple_of(c * share, LANES), share)]
+    block_decay = jnp.exp(-mine * rows)
+    running = jnp.zeros((modes, share), jnp.float32)
+    for d in range(count):
+        ready[d] = running
+
+        @pl.when(d != c)
+        def _():
+            hand_back(d).start()
+            landed(gathered, recv1_sem, d)
+
+        running = running * block_decay + gathered[d]
+    incoming[c] = ready[c]
+    for d in range(count):
+
+        @pl.when(d != c)
+        def _():
+            hand_over(d).wait_send()
+            hand_back(d).wait_send()
+            landed(incoming, recv2_sem, d)
+
+    for k in range(WCUTS):
+        weights(k).start()
+
+    def back_step(d, carry):
+        for h in range(halves):
+            at = pl.ds(pl.multiple_of(d * share + h * LANES, LANES), LANES)
+            state = incoming[d, :, h * LANES : (h + 1) * LANES]
+            far = modal_sum(decay_ref[:, at], coef_ref[:, at] * state, rows, 1.0)
+            whole = jnp.concatenate(far, axis=0) + base_ref[:, at]
+            blocks[here, :, at] = (q_ref[:, at] * whole).astype(jnp.bfloat16)
+        return carry
+
+    lax.fori_loop(0, count, back_step, 0)
 
     def along_z(level, step, sems, k):
         slot = level * 2 + y
@@ -215,8 +279,6 @@
         return act
 
     forward(z, 1, 0)
-    for k in range(WCUTS):
-        weights(k).start()
     for k in range(1, depth):
         both(k, arrive(k))
         both(k - 1, lambda level, step: multiply(level))
@@ -280,6 +342,50 @@
     wide = jnp.einsum("gs,gc->sc", both, spread, precision=lax.Precision.HIGHEST)
     decay_wide, coef_wide = wide[:modes], wide[modes:]
     f32 = jnp.float32
+    cols = out_weight.shape[1]
+    if count == 16 and tps == 2:
+        depth = count // 4
+        dma = pltpu.SemaphoreType.DMA
+        vmem = pl.BlockSpec(memory_space=pltpu.VMEM)
+        out = pl.pallas_call(
+            finish_kernel,
+            in_specs=[vmem] * 7,
+            out_specs=vmem,
+            out_shape=jax.ShapeDtypeStruct((count // 2, rows, cols), jnp.bfloat16),
+            scratch_shapes=[
+                pltpu.VMEM((rows, chans), f32),
+                pltpu.VMEM((rows, chans), f32),
+                pltpu.VMEM((lanes, rows + 8, LANES), f32),
+                pltpu.VMEM((rows + 8, LANES), f32),
+                pltpu.VMEM((rows, LANES), f32),
+                *[pltpu.VMEM((count, modes, chans // count), f32) for _ in range(4)],
+                *[dma((count,)) for _ in range(4)],
+                pltpu.VMEM((2 * depth, rows, chans), jnp.bfloat16),
+                pltpu.VMEM((depth, 2, 2 * rows, cols), f32),
+                pltpu.VMEM((depth, 2 * rows, cols), f32),
+                pltpu.VMEM((depth, 2, rows, cols), jnp.bfloat16),
+                pltpu.VMEM(out_weight.shape, jnp.bfloat16),
+                dma((WCUTS,)),
+                dma((WCUTS,)),
+                dma((depth - 1,)),
+                dma((depth - 1,)),
+                dma((depth,)),
+                dma((depth,)),
+                dma((depth,)),
+                dma((depth,)),
+                dma((depth,)),
+                dma((depth, 2)),
+                dma((count // 2,)),
+            ],
+            compiler_params=pltpu.CompilerParams(
+                collective_id=0, has_side_effects=True, vmem_limit_bytes=40 * 1024 * 1024
+            ),
+            cost_estimate=pl.CostEstimate(
+                flops=2 * 8 * rows * chans * 2 * cols, bytes_accessed=8 * 1024 * 1024, transcendentals=0
+            ),
+            name="finish",
+        )(features, rim, short_weight, decay_wide, coef_wide, skip_gain[None], out_weight)
+        return out.transpose(1, 0, 2).reshape(rows, count // 2 * cols)
     grid = (chans // cb,)
     plane = pl.BlockSpec((rows, cb), lambda i: (0, i))
     modal = pl.BlockSpec((modes, cb), lambda i: (0, i))
@@ -319,43 +425,6 @@
     incoming = lax.all_to_all(
         jnp.concatenate(before, axis=0), "ctx", split_axis=0, concat_axis=1, tiled=True
     )
-    cols = out_weight.shape[1]
-    if count == 16 and tps == 2:
-        depth = count // 4
-        dma = pltpu.SemaphoreType.DMA
-        vmem = pl.BlockSpec(memory_space=pltpu.VMEM)
-        out = pl.pallas_call(
-            finish_kernel,
-            in_specs=[vmem] * 6,
-            out_specs=vmem,
-            out_shape=jax.ShapeDtypeStruct((count // 2, rows, cols), jnp.bfloat16),
-            scratch_shapes=[
-                pltpu.VMEM((2 * depth, rows, chans), jnp.bfloat16),
-                pltpu.VMEM((depth, 2, 2 * rows, cols), f32),
-                pltpu.VMEM((depth, 2 * rows, cols), f32),
-                pltpu.VMEM((depth, 2, rows, cols), jnp.bfloat16),
-                pltpu.VMEM(out_weight.shape, jnp.bfloat16),
-                dma((WCUTS,)),
-                dma((WCUTS,)),
-                dma((depth - 1,)),
-                dma((depth - 1,)),
-                dma((depth,)),
-                dma((depth,)),
-                dma((depth,)),
-                dma((depth,)),
-                dma((depth,)),
-                dma((depth, 2)),
-                dma((count // 2,)),
-            ],
-            compiler_params=pltpu.CompilerParams(
-                collective_id=0, has_side_effects=True, vmem_limit_bytes=40 * 1024 * 1024
-            ),
-            cost_estimate=pl.CostEstimate(
-                flops=2 * 8 * rows * chans * 2 * cols, bytes_accessed=8 * 1024 * 1024, transcendentals=0
-            ),
-            name="finish",
-        )(q, base, incoming, decay_wide, coef_wide, out_weight)
-        return out.transpose(1, 0, 2).reshape(rows, count // 2 * cols)
     mixed = pl.pallas_call(
         back_kernel,
         grid=grid,

time: 115 us -> 90.6 us (0.79)
  blocking collectives: 12.4 us -> 0 us
  waiting for transfers between devices: 7.66 us -> 0.01 us
  Pallas kernels: 73.3 us -> 80.6 us
  local copies, waits for them, and re-layouts: 7.59 us -> 1.82 us
  starting transfers between devices: 9.61 us -> 3.95 us
    all_to_all x1 -> x0, blocking collectives: 12.4 us -> none  [per_device(): lax.all_to_all(jnp.concatenate(before, axis=0), 'ctx', split_axis=0, conc...]
    all_to_all x1 -> x0, waiting for transfers between devices: 7.66 us -> none  [per_device(): pieces = lax.all_to_all(own, 'ctx', split_axis=1, concat_axis=0, tiled=True)]
    pallas_call x2 -> x1, Pallas kernels: 73.3 us -> 80.6 us  [per_device(): pl.pallas_call(finish_kernel, in_specs=[vmem] * 7, out_specs=vmem, out_sh...]
    all_to_all x1 -> x0, starting transfers between devices: 5.66 us -> none  [per_device(): pieces = lax.all_to_all(own, 'ctx', split_axis=1, concat_axis=0, tiled=True)]
    unnamed x11 -> x8, local copies, waits for them, and re-layouts: 2.46 us -> 0.03 us
    all_to_all x2 -> x0, local copies, waits for them, and re-layouts: 1.86 us -> none  [the longest x1 1.85 us: per_device(): pieces = lax.all_to_all(own, 'ctx', split_axis=1, concat_axis=0, tiled=True)]
  transfers between devices with their start and end apart: 2 -> 1, of which waited for: 1 -> 0; matrix products, arithmetic and copies ran while one was open for 3% -> 4% of each run, Pallas kernels for 0% -> 0%
where the time goes in v4:
time: 90.6 us; the launch traced here: 89.7 us
  Pallas kernels  80.6 us (89%)
  starting transfers between devices  3.95 us (4%)
  matrix products  2.46 us (3%)
  local copies, waits for them, and re-layouts  1.82 us (2%)
    pallas_call x1, Pallas kernels, per_device(): pl.pallas_call(finish_kernel, in_specs=[vmem] * 7, out_specs=vmem, out_sh...  80.6 us
    ppermute x1, starting transfers between devices, per_device(): rim = lax.ppermute(features[:, rows - (taps - 1):, :], 'ctx', pairs)  3.95 us
    dot_general x1, matrix products, per_device(): jnp.einsum('gs,gc->sc', both, spread, precision=lax.Precision.HIGHEST)  2.46 us
  transfers between devices with their start and end apart: 1, of which 0 were waited for; matrix products, arithmetic and copies ran while one was open for 4% of the time, Pallas kernels for 0%

profile of v4, /device:TPU:1, one launch (start us, length us, event | category | flops | bytes accessed | tf_op | source)
XLA Modules:
  0.0 89.7 jit_solution(2681446484752970615)
XLA Ops:
  0.0 1.0 %slice.9 = bf16[3,2,4096]{2,1,0:T(2,128)(2,1)S(1)} slice(bf16[3,64,4096]{2,1,0:T(8,128)(2,1)} %x_ref.1), slice={[0:3], [62:64], [0:4096]} | slice | bytes 98304 | tf_op jit(solution)/shard_map/slice | solution.py:334
  1.0 3.9 %collective-permute-start = (bf16[3,2,4096]{2,1,0:T(2,128)(2,1)S(1)}, bf16[3,2,4096]{2,1,0:T(2,128)(2,1)S(1)}, u32[]{:S(2)}, u32[]{:S(2)}) collective-permute-start(bf16[3,2,4096]{2,1,0:T(2,128)(2,1)S(1)} %slice.9), channel_id=1, source_target_pairs={{0,2},{2,4},{4,6},{6,8},{8,10},{10,12},{12,14},{14,16},{16,18},{18... | collective-permute-start | bytes 147464 | tf_op jit(solution)/shard_map/ppermute | solution.py:334
  5.0 0.8 sqrt_multiply_fusion
  5.7 0.0 copy-start
  5.7 0.0 copy-start.1
  5.8 0.0 copy-start.2
  5.8 0.0 copy-start.3
  5.8 2.5 %fusion = f32[32,4096]{1,0:T(8,128)S(1)} fusion(s32[4096]{0:T(1024)S(1)} %get-tuple-element.7, s32[4096]{0:T(1024)S(1)} %get-tuple-element.8, pred[4096]{0:T(1024)(128)(4,1)S(1)} %fusion.9, f32[256,16]{0,1:T(8,128)S(1)} %sqrt_multiply_fusion, f32[256,16]{0,1:T(8,128)} %param.8), kind=kOutput, calls=%fused_computation.1 | convolution fusion | flops 404758528 | bytes 593920 | tf_op jit(solution)/shard_map/gs,gc->sc/dot_general | solution.py:342
  8.3 0.0 collective-permute-done
  8.3 0.1 pad.4.rim_ref
  8.4 0.0 copy-done
  8.4 0.0 copy-done.1
  8.4 0.0 copy-done.2
  8.4 0.0 copy-done.3
  8.4 80.6 %finish.1 = bf16[8,64,256]{2,1,0:T(8,128)(2,1)S(1)} custom-call(bf16[3,64,4096]{2,1,0:T(8,128)(2,1)S(1)} %copy-done, bf16[3,8,4096]{2,1,0:T(8,128)(2,1)S(1)} %pad.4.rim_ref, f32[3,3,4096]{2,1,0:T(4,128)S(1)} %copy-done.2, f32[16,4096]{1,0:T(8,128)S(1)} %get-tuple-element.6.decay_ref, f32[16,4096]{1,0:T(8,128)S(1)} %get-tuple-element.5.coef_ref, ...), custom_call_target="tpu_custom_call" | custom-call | flops 2147483648 | bytes 8388608 | tf_op jit(solution)/shard_map/finish/pallas_call | solution.py:350
  89.0 0.7 copy.8
  (3 shorter events, 0.1 us)
Async XLA Ops:
  1.0 7.3 %collective-permute-start = (bf16[3,2,4096]{2,1,0:T(2,128)(2,1)S(1)}, bf16[3,2,4096]{2,1,0:T(2,128)(2,1)S(1)}, u32[]{:S(2)}, u32[]{:S(2)}) collective-permute-start(bf16[3,2,4096]{2,1,0:T(2,128)(2,1)S(1)} %slice.9), channel_id=1, source_target_pairs={{0,2},{2,4},{4,6},{6,8},{8,10},{10,12},{12,14},{14,16},{16,18},{18... | collective-permute-start | bytes 147464 | tf_op jit(solution)/shard_map/ppermute | solution.py:334
  5.7 2.6 %copy-start = (bf16[3,64,4096]{2,1,0:T(8,128)(2,1)S(1)}, bf16[3,64,4096]{2,1,0:T(8,128)(2,1)}, u32[]{:S(2)}) copy-start(bf16[3,64,4096]{2,1,0:T(8,128)(2,1)} %x_ref.1) | copy-start | bytes 4718596
  5.7 2.6 %copy-start.1 = (bf16[4096,256]{1,0:T(8,128)(2,1)S(1)}, bf16[4096,256]{1,0:T(8,128)(2,1)}, u32[]{:S(2)}) copy-start(bf16[4096,256]{1,0:T(8,128)(2,1)} %own_ref.1) | copy-start | bytes 6291460
  5.8 2.6 %copy-start.2 = (f32[3,3,4096]{2,1,0:T(4,128)S(1)}, f32[3,3,4096]{2,1,0:T(4,128)}, u32[]{:S(2)}) copy-start(f32[3,3,4096]{2,1,0:T(4,128)} %w_ref.1) | copy-start | bytes 442372
  5.8 2.6 %copy-start.3 = (f32[4096]{0:T(1024)S(1)}, f32[4096]{0:T(1024)}, u32[]{:S(2)}) copy-start(f32[4096]{0:T(1024)} %param.10) | copy-start | bytes 49156

commit v5 on v4

--- a/solution.py
+++ b/solution.py
@@ -7,6 +7,7 @@
 
 LANES = 128
 WCUTS = 4
+PARTS = 2
 
 
 def modal_sum(decay, weight, rows, shift):
@@ -156,6 +157,7 @@
 
         return carry
 
+    weights(0).start()
     lax.fori_loop(0, count, front_step, 0)
     gathered[c] = ends[c]
     mine = decay_ref[:, pl.ds(pl.multiple_of(c * share, LANES), share)]
@@ -179,7 +181,7 @@
             hand_back(d).wait_send()
             landed(incoming, recv2_sem, d)
 
-    for k in range(WCUTS):
+    for k in range(1, WCUTS):
         weights(k).start()
 
     def back_step(d, carry):
@@ -191,19 +193,22 @@
             blocks[here, :, at] = (q_ref[:, at] * whole).astype(jnp.bfloat16)
         return carry
 
-    lax.fori_loop(0, count, back_step, 0)
-
-    def along_z(level, step, sems, k):
-        slot = level * 2 + y
-        return pltpu.make_async_remote_copy(
-            blocks.at[slot], blocks.at[slot], sems.at[k], z_sem.at[level],
+    part_lanes = blocks.shape[2] // PARTS
+
+    def piece(slot, h):
+        return blocks.at[slot, :, pl.ds(h * part_lanes, part_lanes)]
+
+    def along_z(level, step, sems, k, h):
+        part = piece(level * 2 + y, h)
+        return pltpu.make_async_remote_copy(
+            part, part, sems.at[k, h], z_sem.at[level, h],
             device_id=(c + 4 * step, p), device_id_type=mesh_ids,
         )
 
-    def along_y(level):
-        slot = level * 2 + y
-        return pltpu.make_async_remote_copy(
-            blocks.at[slot], blocks.at[slot], ysend_sem.at[level], yrecv_sem.at[level],
+    def along_y(level, h):
+        part = piece(level * 2 + y, h)
+        return pltpu.make_async_remote_copy(
+            part, part, ysend_sem.at[level, h], yrecv_sem.at[level, h],
             device_id=(c + 2 - 4 * y, p), device_id_type=mesh_ids,
         )
 
@@ -223,9 +228,16 @@
         )
 
     def multiply(level):
-        pltpu.make_async_copy(blocks.at[level * 2 + 1 - y], blocks.at[level * 2 + 1 - y], yrecv_sem.at[level]).wait()
+        for h in range(PARTS):
+            part = piece(level * 2 + 1 - y, h)
+            pltpu.make_async_copy(part, part, yrecv_sem.at[level, h]).wait()
         lhs = blocks[pl.ds(level * 2, 2)].reshape(2 * rows, blocks.shape[2])
         result[level, x] = jnp.dot(lhs, own_ref[...], preferred_element_type=jnp.float32)
+
+    def multiply_pair(level):
+        lhs = blocks[pl.ds(level * 2, 2)].reshape(2 * rows, blocks.shape[2])
+        result[level, 1 - x] = jnp.dot(lhs, pair[...], preferred_element_type=jnp.float32)
+        to_core(level).start()
 
     def deliver(level):
         to_core(level).wait_recv()
@@ -255,47 +267,55 @@
 
     can_up, can_down = z + 1 < depth, z >= 1
 
-    def forward(level, step, k):
+    def forward(level, step, k, h):
         if k + 1 < depth:
             if step > 0 or k == 0:
 
                 @pl.when(can_up)
                 def _():
-                    along_z(level, 1, up_sem, k).start()
+                    along_z(level, 1, up_sem, k, h).start()
 
             if step < 0 or k == 0:
 
                 @pl.when(can_down)
                 def _():
-                    along_z(level, -1, down_sem, k).start()
-
-        along_y(level).start()
+                    along_z(level, -1, down_sem, k, h).start()
+
+        along_y(level, h).start()
 
     def arrive(k):
         def act(level, step):
-            pltpu.make_async_copy(blocks.at[level * 2 + y], blocks.at[level * 2 + y], z_sem.at[level]).wait()
-            forward(level, step, k)
+            for h in range(PARTS):
+                part = piece(level * 2 + y, h)
+                pltpu.make_async_copy(part, part, z_sem.at[level, h]).wait()
+                forward(level, step, k, h)
 
         return act
 
-    forward(z, 1, 0)
+    per = count // PARTS
+    for h in range(PARTS):
+        lax.fori_loop(h * per, (h + 1) * per, back_step, 0)
+        forward(z, 1, 0, h)
     for k in range(1, depth):
         both(k, arrive(k))
+        if k == depth - 1:
+            for j in range(WCUTS):
+                weights(j).wait()
+            for j in range(k - 1):
+                both(j, lambda level, step: multiply_pair(level))
         both(k - 1, lambda level, step: multiply(level))
+        if k == depth - 1:
+            both(k - 1, lambda level, step: multiply_pair(level))
+            for j in range(k - 1):
+                both(j, lambda level, step: deliver(level))
     both(depth - 1, lambda level, step: multiply(level))
-    for k in range(WCUTS):
-        weights(k).wait()
-        lhs = blocks[:, :, k * span : (k + 1) * span].reshape(2 * depth * rows, span)
-        term = jnp.dot(lhs, pair[k * span : (k + 1) * span], preferred_element_type=jnp.float32)
-        term = term.reshape(depth, 2 * rows, term.shape[1])
-        result[:, 1 - x] = term if k == 0 else result[:, 1 - x] + term
+    both(depth - 1, lambda level, step: multiply_pair(level))
+    both(depth - 2, lambda level, step: deliver(level))
+    both(depth - 1, lambda level, step: deliver(level))
+
     for level in range(depth):
-        to_core(level).start()
-    for level in range(depth):
-        deliver(level)
-
-    for level in range(depth):
-        along_y(level).wait_send()
+        for h in range(PARTS):
+            along_y(level, h).wait_send()
         to_core(level).wait_send()
         for far_y in range(2):
             mine = jnp.logical_and(jnp.logical_and(level == z, far_y == y), side == p)
@@ -308,11 +328,13 @@
 
         @pl.when(jnp.logical_and(z - k >= 0, can_up))
         def _():
-            along_z(z - k, 1, up_sem, k).wait_send()
+            for h in range(PARTS):
+                along_z(z - k, 1, up_sem, k, h).wait_send()
 
         @pl.when(jnp.logical_and(z + k < depth, can_down))
         def _():
-            along_z(z + k, -1, down_sem, k).wait_send()
+            for h in range(PARTS):
+                along_z(z + k, -1, down_sem, k, h).wait_send()
 
     for source in range(out_ref.shape[0]):
 
@@ -367,11 +389,11 @@
                 pltpu.VMEM(out_weight.shape, jnp.bfloat16),
                 dma((WCUTS,)),
                 dma((WCUTS,)),
-                dma((depth - 1,)),
-                dma((depth - 1,)),
-                dma((depth,)),
-                dma((depth,)),
-                dma((depth,)),
+                dma((depth - 1, PARTS)),
+                dma((depth - 1, PARTS)),
+                dma((depth, PARTS)),
+                dma((depth, PARTS)),
+                dma((depth, PARTS)),
                 dma((depth,)),
                 dma((depth,)),
                 dma((depth, 2)),

time: 90.6 us -> 96.2 us (1.062)
  Pallas kernels: 80.6 us -> 86.7 us
    pallas_call x1, Pallas kernels: 80.6 us -> 86.7 us  [per_device(): pl.pallas_call(finish_kernel, in_specs=[vmem] * 7, out_specs=vmem, out_sh...]
  transfers between devices with their start and end apart: 1 -> 1, of which waited for: 0 -> 0; matrix products, arithmetic and copies ran while one was open for 4% -> 3% of each run, Pallas kernels for 0% -> 0%
where the time goes in v5:
time: 96.2 us; the launch traced here: 95.8 us
  Pallas kernels  86.7 us (90%)
  starting transfers between devices  3.95 us (4%)
  matrix products  2.46 us (3%)
  local copies, waits for them, and re-layouts  1.82 us (2%)
    pallas_call x1, Pallas kernels, per_device(): pl.pallas_call(finish_kernel, in_specs=[vmem] * 7, out_specs=vmem, out_sh...  86.7 us
    ppermute x1, starting transfers between devices, per_device(): rim = lax.ppermute(features[:, rows - (taps - 1):, :], 'ctx', pairs)  3.95 us
    dot_general x1, matrix products, per_device(): jnp.einsum('gs,gc->sc', both, spread, precision=lax.Precision.HIGHEST)  2.46 us
  transfers between devices with their start and end apart: 1, of which 0 were waited for; matrix products, arithmetic and copies ran while one was open for 3% of the time, Pallas kernels for 0%

profile of v5, /device:TPU:1, one launch (start us, length us, event | category | flops | bytes accessed | tf_op | source)
XLA Modules:
  0.0 95.8 jit_solution(5766848030365191129)
XLA Ops:
  0.0 1.0 %slice.9 = bf16[3,2,4096]{2,1,0:T(2,128)(2,1)S(1)} slice(bf16[3,64,4096]{2,1,0:T(8,128)(2,1)} %x_ref.1), slice={[0:3], [62:64], [0:4096]} | slice | bytes 98304 | tf_op jit(solution)/shard_map/slice | solution.py:356
  1.0 3.9 %collective-permute-start = (bf16[3,2,4096]{2,1,0:T(2,128)(2,1)S(1)}, bf16[3,2,4096]{2,1,0:T(2,128)(2,1)S(1)}, u32[]{:S(2)}, u32[]{:S(2)}) collective-permute-start(bf16[3,2,4096]{2,1,0:T(2,128)(2,1)S(1)} %slice.9), channel_id=1, source_target_pairs={{0,2},{2,4},{4,6},{6,8},{8,10},{10,12},{12,14},{14,16},{16,18},{18... | collective-permute-start | bytes 147464 | tf_op jit(solution)/shard_map/ppermute | solution.py:356
  5.0 0.8 sqrt_multiply_fusion
  5.7 0.0 copy-start
  5.7 0.0 copy-start.1
  5.8 0.0 copy-start.2
  5.8 0.0 copy-start.3
  5.8 2.5 %fusion = f32[32,4096]{1,0:T(8,128)S(1)} fusion(s32[4096]{0:T(1024)S(1)} %get-tuple-element.7, s32[4096]{0:T(1024)S(1)} %get-tuple-element.8, pred[4096]{0:T(1024)(128)(4,1)S(1)} %fusion.9, f32[256,16]{0,1:T(8,128)S(1)} %sqrt_multiply_fusion, f32[256,16]{0,1:T(8,128)} %param.8), kind=kOutput, calls=%fused_computation.1 | convolution fusion | flops 404758528 | bytes 593920 | tf_op jit(solution)/shard_map/gs,gc->sc/dot_general | solution.py:364
  8.3 0.0 collective-permute-done
  8.3 0.1 pad.4.rim_ref
  8.4 0.0 copy-done
  8.4 0.0 copy-done.1
  8.4 0.0 copy-done.2
  8.4 0.0 copy-done.3
  8.4 86.7 %finish.1 = bf16[8,64,256]{2,1,0:T(8,128)(2,1)S(1)} custom-call(bf16[3,64,4096]{2,1,0:T(8,128)(2,1)S(1)} %copy-done, bf16[3,8,4096]{2,1,0:T(8,128)(2,1)S(1)} %pad.4.rim_ref, f32[3,3,4096]{2,1,0:T(4,128)S(1)} %copy-done.2, f32[16,4096]{1,0:T(8,128)S(1)} %get-tuple-element.6.decay_ref, f32[16,4096]{1,0:T(8,128)S(1)} %get-tuple-element.5.coef_ref, ...), custom_call_target="tpu_custom_call" | custom-call | flops 2147483648 | bytes 8388608 | tf_op jit(solution)/shard_map/finish/pallas_call | solution.py:372
  95.1 0.7 copy.8
  (3 shorter events, 0.1 us)
Async XLA Ops:
  1.0 7.3 %collective-permute-start = (bf16[3,2,4096]{2,1,0:T(2,128)(2,1)S(1)}, bf16[3,2,4096]{2,1,0:T(2,128)(2,1)S(1)}, u32[]{:S(2)}, u32[]{:S(2)}) collective-permute-start(bf16[3,2,4096]{2,1,0:T(2,128)(2,1)S(1)} %slice.9), channel_id=1, source_target_pairs={{0,2},{2,4},{4,6},{6,8},{8,10},{10,12},{12,14},{14,16},{16,18},{18... | collective-permute-start | bytes 147464 | tf_op jit(solution)/shard_map/ppermute | solution.py:356
  5.7 2.6 %copy-start = (bf16[3,64,4096]{2,1,0:T(8,128)(2,1)S(1)}, bf16[3,64,4096]{2,1,0:T(8,128)(2,1)}, u32[]{:S(2)}) copy-start(bf16[3,64,4096]{2,1,0:T(8,128)(2,1)} %x_ref.1) | copy-start | bytes 4718596
  5.7 2.6 %copy-start.1 = (bf16[4096,256]{1,0:T(8,128)(2,1)S(1)}, bf16[4096,256]{1,0:T(8,128)(2,1)}, u32[]{:S(2)}) copy-start(bf16[4096,256]{1,0:T(8,128)(2,1)} %own_ref.1) | copy-start | bytes 6291460
  5.8 2.6 %copy-start.2 = (f32[3,3,4096]{2,1,0:T(4,128)S(1)}, f32[3,3,4096]{2,1,0:T(4,128)}, u32[]{:S(2)}) copy-start(f32[3,3,4096]{2,1,0:T(4,128)} %w_ref.1) | copy-start | bytes 442372
  5.8 2.6 %copy-start.3 = (f32[4096]{0:T(1024)S(1)}, f32[4096]{0:T(1024)}, u32[]{:S(2)}) copy-start(f32[4096]{0:T(1024)} %param.10) | copy-start | bytes 49156
